TPU v7x, 128 devices: a whole 4x4x4 slice. The times are simulated.
128 devices in a mesh: fsdp: 16 (over y, x), tp: 8 (over z, core).
Axes of the slice: x: 4, y: 4, z: 4, core: 2. Of those that a mesh axis runs over, the one named last changes fastest.
Arguments:
- gradient: bfloat16 [8192, 10240], P(('fsdp', 'tp'))
- owner: int32 [80], replicated, may hold values from 0 to 127, as said below
- l_stat: float32 [128, 1024, 1024], P(('fsdp', 'tp'))
- r_stat: float32 [128, 1024, 1024], P(('fsdp', 'tp'))
- l_root: bfloat16 [128, 1024, 1024], P(('fsdp', 'tp'))
- r_root: bfloat16 [128, 1024, 1024], P(('fsdp', 'tp'))
Outputs:
- update: bfloat16 [8192, 10240], P('fsdp', 'tp')
- new_left: float32 [128, 1024, 1024], P(('fsdp', 'tp'))
- new_right: float32 [128, 1024, 1024], P(('fsdp', 'tp'))
Inputs may be any that keep to these rules, and one draw needn't show every extreme that they name: `owner`: no two blocks name the same slot; slot g lies on device g, devices numbered fsdp index times the size of tp plus tp index. Among the 10 blocks of one row of blocks at most 1 have owners with the same fsdp index, and some row of blocks has exactly 1 such.
All inputs are finite; a program needn't handle non-finite values.
Results may differ from a plain program's by a relative error of at most 0.0049.
Values may be sent and summed in bfloat16 or wider, within the bound.
A program may use at most 128 MiB of HBM per device.

v0:
```python
from functools import partial

import jax
import jax.numpy as jnp
from jax import lax
from jax.sharding import PartitionSpec as P

decay = 0.9
eps = 1e-06


def ranks_of(owner_line, per_fsdp):
    fsdp_of = owner_line // per_fsdp
    count = owner_line.shape[0]
    earlier = jnp.arange(count)[None, :] < jnp.arange(count)[:, None]
    same_fsdp = fsdp_of[None, :] == fsdp_of[:, None]
    ranking = jnp.sum((earlier & same_fsdp).astype(jnp.int32), axis=1)
    return (fsdp_of, ranking)


def precondition(blocks, l_stat, r_stat, l_root, r_root):
    left_new = decay * l_stat + (1.0 - decay) * jnp.einsum(
        "sij,skj->sik", blocks, blocks, preferred_element_type=jnp.float32
    )
    right_new = decay * r_stat + (1.0 - decay) * jnp.einsum(
        "sji,sjk->sik", blocks, blocks, preferred_element_type=jnp.float32
    )
    halfway = jnp.einsum("sij,sjk->sik", l_root, blocks, preferred_element_type=jnp.float32).astype(
        jnp.bfloat16
    )
    product = jnp.einsum("sij,sjk->sik", halfway, r_root, preferred_element_type=jnp.float32)
    factor = lax.rsqrt(jnp.mean(product * product, axis=(1, 2), keepdims=True) + eps)
    return ((product * factor).astype(jnp.bfloat16), left_new, right_new)


def per_device(gradient, owner, l_stat, r_stat, l_root, r_root):
    shard_rows, total_cols = gradient.shape
    slot_count = l_stat.shape[0]
    block_size = l_stat.shape[1]
    tp_count = lax.axis_size("tp")
    fsdp_count = lax.axis_size("fsdp")
    device_count = tp_count * fsdp_count
    column_blocks = total_cols // block_size
    group_size = block_size // shard_rows
    row_blocks = device_count // group_size
    my_fsdp = lax.axis_index("fsdp")
    my_index = my_fsdp * tp_count + lax.axis_index("tp")
    my_block_row = my_index // group_size
    owner_line = lax.dynamic_slice_in_dim(owner, my_block_row * column_blocks, column_blocks)
    pieces = gradient.reshape(shard_rows, column_blocks, block_size)
    per_fsdp = tp_count * slot_count
    part_rows = block_size // (shard_rows * tp_count)
    capacity = -(-column_blocks // fsdp_count)
    owner_fsdp, owner_rank = ranks_of(owner_line, per_fsdp)
    select_rows = (
        (owner_fsdp[None, None, :] == jnp.arange(fsdp_count)[:, None, None])
        & (owner_rank[None, None, :] == jnp.arange(capacity)[None, :, None])
    ).astype(jnp.bfloat16)
    outgoing = jnp.einsum(
        "fkc,rcb->fkrb", select_rows, pieces, preferred_element_type=jnp.float32
    ).astype(jnp.bfloat16)
    arrived = lax.all_to_all(outgoing, "fsdp", split_axis=0, concat_axis=0, tiled=True)
    table = jnp.repeat(owner.reshape(row_blocks, column_blocks), part_rows, axis=0)
    table_fsdp, table_rank = jax.vmap(partial(ranks_of, per_fsdp=per_fsdp))(table)
    table_tp = table // slot_count % tp_count
    table_slot = table % slot_count
    source_part = jnp.arange(fsdp_count) % part_rows
    matched = (table_fsdp == my_fsdp)[None, None, None, :, None, :]
    matched = matched & (
        table_rank[None, None, None, :, None, :]
        == jnp.arange(capacity)[None, None, None, None, :, None]
    )
    matched = matched & (
        table_tp[None, None, None, :, None, :]
        == jnp.arange(tp_count)[:, None, None, None, None, None]
    )
    matched = matched & (
        table_slot[None, None, None, :, None, :]
        == jnp.arange(slot_count)[None, :, None, None, None, None]
    )
    matched = matched & (
        source_part[None, None, None, :, None, None]
        == jnp.arange(part_rows)[None, None, :, None, None, None]
    )
    routing = jnp.sum(matched.astype(jnp.int32), axis=5).astype(jnp.bfloat16)
    forward = jnp.einsum(
        "tspfk,fkrb->tsprb", routing, arrived, preferred_element_type=jnp.float32
    ).astype(jnp.bfloat16)
    forward = forward.reshape(tp_count, slot_count, part_rows, 1, shard_rows, block_size)
    collected = lax.all_to_all(forward, "tp", split_axis=0, concat_axis=3, tiled=True)
    blocks = collected.reshape(slot_count, block_size, block_size)
    scaled, new_left, new_right = precondition(blocks, l_stat, r_stat, l_root, r_root)
    spread_out = scaled.reshape(slot_count, part_rows, tp_count, shard_rows, block_size)
    returned = lax.all_to_all(spread_out, "tp", split_axis=2, concat_axis=2, tiled=True)
    backward = jnp.einsum(
        "tspfk,sptrb->fkrb", routing, returned, preferred_element_type=jnp.float32
    ).astype(jnp.bfloat16)
    homeward = lax.all_to_all(backward, "fsdp", split_axis=0, concat_axis=0, tiled=True)
    row_pieces = jnp.einsum(
        "fkc,fkrb->rcb", select_rows, homeward, preferred_element_type=jnp.float32
    )
    row_major = row_pieces.astype(jnp.bfloat16).reshape(shard_rows, total_cols)
    update = lax.all_to_all(row_major, "tp", split_axis=1, concat_axis=0, tiled=True)
    return (update, new_left, new_right)


def solution(mesh):
    return jax.shard_map(
        per_device,
        mesh=mesh,
        in_specs=(
            P(("fsdp", "tp"), None),
            P(),
            P(("fsdp", "tp"), None, None),
            P(("fsdp", "tp"), None, None),
            P(("fsdp", "tp"), None, None),
            P(("fsdp", "tp"), None, None),
        ),
        out_specs=(P("fsdp", "tp"), P(("fsdp", "tp"), None, None), P(("fsdp", "tp"), None, None)),
        check_vma=False,
    )
```

profile of v0, /device:TPU:1, one launch (start us, length us, event | category | flops | bytes accessed | tf_op | source)
XLA Modules:
  0.0 199.8 jit_solution(4803161293772709012)
XLA Ops:
  1.7 3.6 %reshape.379 = bf16[64,10,1024]{2,1,0:T(8,128)(2,1)} reshape(bf16[64,10240]{1,0:T(8,128)(2,1)} %param.6) | data formatting | bytes 2621440 | tf_op jit(solution)/shard_map/reshape | solution.py:50
  5.3 2.4 %convert_bitcast_fusion.2 = bf16[16,1,64,1024]{3,0,2,1:T(8,128)(2,1)S(1)} fusion(bf16[64,10,1024]{2,1,0:T(8,128)(2,1)} %reshape.379, s32[10]{0:T(128)S(1)} %and_select_fusion, pred[10]{0:T(512)(128)(4,1)S(1)} %broadcast_compare_fusion), kind=kOutput, calls=%fused_computation.23 | convolution fusion | flops 22020416 | bytes 3407922 | tf_op jit(solution)/shard_map/fkc,rcb->fkrb/dot_general | solution.py:59
  7.7 2.5 %copy.53 = bf16[16,1,64,1024]{3,2,1,0:T(8,128)(2,1)} copy(bf16[16,1,64,1024]{3,0,2,1:T(8,128)(2,1)S(1)} %convert_bitcast_fusion.2) | data formatting | bytes 4194304 | tf_op jit(solution)/shard_map/convert_element_type | solution.py:61
  10.2 7.8 %all-to-all-start = ((bf16[16,1,64,1024]{3,2,1,0:T(8,128)(2,1)}), bf16[16,1,64,1024]{3,2,1,0:T(8,128)(2,1)}, u32[]{:S(2)}, u32[]{:S(2)}) async-start(bf16[16,1,64,1024]{3,2,1,0:T(8,128)(2,1)} %copy.53), calls=%async_computation | async-start | bytes 4194304 | tf_op jit(solution)/shard_map/all_to_all | solution.py:62
  18.7 29.8 %all-to-all-done = bf16[16,1,64,1024]{3,2,1,0:T(8,128)(2,1)} async-done(((bf16[16,1,64,1024]{3,2,1,0:T(8,128)(2,1)}), bf16[16,1,64,1024]{3,2,1,0:T(8,128)(2,1)}, u32[]{:S(2)}, u32[]{:S(2)}) %all-to-all-start) | async-done | bytes 2097184 | tf_op jit(solution)/shard_map/all_to_all | solution.py:62
  48.5 3.1 %convert_bitcast_fusion.1 = bf16[8,1,2,1,64,1024]{5,0,4,2,3,1:T(8,128)(2,1)S(1)} fusion(bf16[16,1,64,1024]{3,2,1,0:T(8,128)(2,1)} %all-to-all-done, s32[8,2,16]{2,0,1:T(8,128)S(1)} %convert_reduce_fusion), kind=kOutput, calls=%fused_computation.22 | convolution fusion | flops 34603264 | bytes 4195328 | tf_op jit(solution)/shard_map/tspfk,fkrb->tsprb/dot_general | solution.py:86
  51.6 1.2 copy.55
  52.8 33.7 %all_to_all.49 = bf16[8,1,2,1,64,1024]{5,4,2,3,1,0:T(8,128)(2,1)S(1)} all-to-all(bf16[8,1,2,1,64,1024]{5,4,2,3,1,0:T(8,128)(2,1)S(1)} %copy.55), channel_id=1, replica_groups=mesh['fsdp'=16,'tp'=8] {'tp'}, dimensions={0} | all-to-all | bytes 4194304 | tf_op jit(solution)/shard_map/all_to_all | solution.py:90
  86.5 1.2 copy.91
  87.9 2.5 %copy.57 = bf16[1,1,2,8,1,64,1024]{6,5,3,2,4,1,0:T(8,128)(2,1)} copy(bf16[1,1,2,8,1,64,1024]{6,3,5,2,4,1,0:T(8,128)(2,1)S(1)} %bitcast.91) | data formatting | bytes 4194304 | tf_op jit(solution)/shard_map/all_to_all | solution.py:90
  90.3 9.5 %multiply_reduce_fusion = (f32[]{:T(128)}, f32[1024,1024]{1,0:T(8,128)}) fusion(bf16[1,1024,1024]{2,1,0:T(8,128)(2,1)S(1)} %copy-done, bf16[1024,1024]{1,0:T(8,128)(2,1)} %bitcast.93, bf16[1,1024,1024]{2,1,0:T(8,128)(2,1)} %param.10), kind=kOutput, calls=%fused_computation.6 | convolution fusion | flops 4298113024 | bytes 10485764 | tf_op jit(solution)/shard_map/sij,sjk->sik/dot_general | solution.py:31
  100.5 2.8 %multiply_convert_fusion = bf16[1024,1024]{1,0:T(8,128)(2,1)S(1)} fusion(f32[1024,1024]{1,0:T(8,128)} %get-tuple-element.6, f32[]{:T(128)S(6)} %rsqrt.4), kind=kLoop, calls=%fused_computation.5 | loop fusion | flops 2097152 | bytes 6291460 | tf_op jit(solution)/shard_map/convert_element_type | solution.py:33
  103.3 2.2 %copy.58 = bf16[1,2,8,64,1024]{4,1,3,0,2:T(2,128)(2,1)S(1)} copy(bf16[1,2,8,64,1024]{4,3,2,1,0:T(8,128)(2,1)S(1)} %bitcast.90) | data formatting | bytes 4194304 | tf_op jit(solution)/shard_map/reshape | solution.py:93
  105.5 30.0 %all_to_all.50 = bf16[1,2,8,64,1024]{4,1,3,0,2:T(2,128)(2,1)S(1)} all-to-all(bf16[1,2,8,64,1024]{4,1,3,0,2:T(2,128)(2,1)S(1)} %copy.58), channel_id=1, replica_groups=mesh['fsdp'=16,'tp'=8] {'tp'}, dimensions={2} | all-to-all | bytes 4194304 | tf_op jit(solution)/shard_map/all_to_all | solution.py:94
  135.4 1.3 fusion.21
  136.8 1.2 copy.60
  137.9 30.2 %all_to_all.51 = bf16[16,1,64,1024]{3,2,1,0:T(8,128)(2,1)S(1)} all-to-all(bf16[16,1,64,1024]{3,2,1,0:T(8,128)(2,1)S(1)} %copy.60), channel_id=1, replica_groups=mesh['fsdp'=16,'tp'=8] {'fsdp'}, dimensions={0} | all-to-all | bytes 4194304 | tf_op jit(solution)/shard_map/all_to_all | solution.py:98
  168.1 2.8 %convert_bitcast_fusion = bf16[64,10,1024]{2,1,0:T(8,128)(2,1)} fusion(bf16[16,1,64,1024]{3,2,1,0:T(8,128)(2,1)S(1)} %all_to_all.51, s32[10]{0:T(128)S(1)} %and_select_fusion, pred[10]{0:T(512)(128)(4,1)S(1)} %broadcast_compare_fusion), kind=kOutput, calls=%fused_computation.20 | convolution fusion | flops 21627200 | bytes 3407922 | tf_op jit(solution)/shard_map/fkc,fkrb->rcb/dot_general | solution.py:99
  170.9 3.0 %all_to_all.40 = bf16[64,8,1280]{2,1,0:T(8,128)(2,1)S(1)} reshape(bf16[64,10,1024]{2,1,0:T(8,128)(2,1)} %convert_bitcast_fusion) | data formatting | bytes 2621440 | tf_op jit(solution)/shard_map/all_to_all | solution.py:103
  173.9 1.3 copy.62
  175.2 5.7 %all-to-all-start.4 = ((bf16[64,8,1280]{2,0,1:T(8,128)(2,1)}), bf16[64,8,1280]{2,0,1:T(8,128)(2,1)S(1)}, u32[]{:S(2)}, u32[]{:S(2)}) async-start(bf16[64,8,1280]{2,0,1:T(8,128)(2,1)} %copy.62), calls=%async_computation.4 | async-start | bytes 2621440 | tf_op jit(solution)/shard_map/all_to_all | solution.py:103
  180.8 9.3 %fusion.1 = f32[1,1024,1024]{2,1,0:T(8,128)} fusion(f32[1,1024,1024]{2,1,0:T(8,128)} %param.9, bf16[8,1,2,1,64,1024]{5,4,2,3,1,0:T(8,128)(2,1)} %copy-done.1), kind=kOutput, calls=%fused_computation.2 | convolution fusion | flops 2150629376 | bytes 10485760 | tf_op jit(solution)/shard_map/sji,sjk->sik/dot_general | solution.py:25
  190.2 4.5 %bitcast_add_fusion = f32[1,1024,1024]{2,1,0:T(8,128)} fusion(f32[1,1024,1024]{2,1,0:T(8,128)S(1)} %copy-done.4, bf16[1024,1024]{1,0:T(8,128)(2,1)S(1)} %bitcast.94), kind=kOutput, calls=%fused_computation.3 | convolution fusion | flops 2150629376 | bytes 10485760 | tf_op jit(solution)/shard_map/sij,skj->sik/dot_general | solution.py:22
  194.7 4.1 %all-to-all-done.4 = bf16[64,8,1280]{2,0,1:T(8,128)(2,1)S(1)} async-done(((bf16[64,8,1280]{2,0,1:T(8,128)(2,1)}), bf16[64,8,1280]{2,0,1:T(8,128)(2,1)S(1)}, u32[]{:S(2)}, u32[]{:S(2)}) %all-to-all-start.4) | async-done | bytes 1310752 | tf_op jit(solution)/shard_map/all_to_all | solution.py:103
  (26 shorter events, 3.0 us)
Async XLA Ops:
  0.6 89.7 %copy-start = (bf16[1,1024,1024]{2,1,0:T(8,128)(2,1)S(1)}, bf16[1,1024,1024]{2,1,0:T(8,128)(2,1)}, u32[]{:S(2)}) copy-start(bf16[1,1024,1024]{2,1,0:T(8,128)(2,1)} %param.11) | copy-start | bytes 6291460
  10.2 7.8 %copy-start.3 = (s32[80]{0:T(128)S(1)}, s32[80]{0:T(128)}, u32[]{:S(2)}) copy-start(s32[80]{0:T(128)} %param.7) | copy-start | bytes 964
  10.2 38.3 %all-to-all-start = ((bf16[16,1,64,1024]{3,2,1,0:T(8,128)(2,1)}), bf16[16,1,64,1024]{3,2,1,0:T(8,128)(2,1)}, u32[]{:S(2)}, u32[]{:S(2)}) async-start(bf16[16,1,64,1024]{3,2,1,0:T(8,128)(2,1)} %copy.53), calls=%async_computation | async-start | bytes 4194304 | tf_op jit(solution)/shard_map/all_to_all | solution.py:62
  86.5 1.4 copy-start.1
  175.2 23.6 %all-to-all-start.4 = ((bf16[64,8,1280]{2,0,1:T(8,128)(2,1)}), bf16[64,8,1280]{2,0,1:T(8,128)(2,1)S(1)}, u32[]{:S(2)}, u32[]{:S(2)}) async-start(bf16[64,8,1280]{2,0,1:T(8,128)(2,1)} %copy.62), calls=%async_computation.4 | async-start | bytes 2621440 | tf_op jit(solution)/shard_map/all_to_all | solution.py:103
  180.8 9.3 %copy-start.2 = (bf16[1,1,2,8,1,64,1024]{6,5,3,2,4,1,0:T(8,128)(2,1)S(1)}, bf16[1,1,2,8,1,64,1024]{6,5,3,2,4,1,0:T(8,128)(2,1)}, u32[]{:S(2)}) copy-start(bf16[1,1,2,8,1,64,1024]{6,5,3,2,4,1,0:T(8,128)(2,1)} %copy.57) | copy-start | bytes 6291460
  180.8 9.3 %copy-start.4 = (f32[1,1024,1024]{2,1,0:T(8,128)S(1)}, f32[1,1024,1024]{2,1,0:T(8,128)}, u32[]{:S(2)}) copy-start(f32[1,1024,1024]{2,1,0:T(8,128)} %param.8) | copy-start | bytes 12582916
where the time goes:
time: 200 us
  blocking collectives  93.9 us (47%)
  waiting for transfers between devices  33.9 us (17%)
  matrix products  33 us (16%)
  local copies, waits for them, and re-layouts  19.9 us (10%)
  starting transfers between devices  13.4 us (7%)
  other arithmetic  4.24 us (2%)
    all_to_all x1, blocking collectives, per_device(): lax.all_to_all(forward, 'tp', split_axis=0, concat_axis=3, tiled=True)  33.7 us
    all_to_all x1, blocking collectives, per_device(): lax.all_to_all(backward, 'fsdp', split_axis=0, concat_axis=0, tiled=True)  30.2 us
    all_to_all x1, blocking collectives, per_device(): lax.all_to_all(spread_out, 'tp', split_axis=2, concat_axis=2, tiled=True)  30 us
    all_to_all x1, waiting for transfers between devices, per_device(): lax.all_to_all(outgoing, 'fsdp', split_axis=0, concat_axis=0, tiled=True)  29.8 us
    dot_general x1, matrix products, precondition(): jnp.einsum('sij,sjk->sik', halfway, r_root, preferred_element_type=jnp.fl...  9.52 us
    dot_general x1, matrix products, precondition(): jnp.einsum('sji,sjk->sik', blocks, blocks, preferred_element_type=jnp.flo...  9.34 us
    all_to_all x1, starting transfers between devices, per_device(): lax.all_to_all(outgoing, 'fsdp', split_axis=0, concat_axis=0, tiled=True)  7.77 us
    all_to_all x1, starting transfers between devices, per_device(): lax.all_to_all(row_major, 'tp', split_axis=1, concat_axis=0, tiled=True)  5.68 us
  transfers between devices with their start and end apart: 2, of which 2 were waited for; matrix products, arithmetic and copies ran while one was open for 7% of the time, Pallas kernels for 0%

commit v1 on v0

v1 whole, which is shorter than its diff:
```python
import functools

import jax
import jax.numpy as jnp
from jax import lax
from jax.experimental import pallas as pl
from jax.experimental.pallas import tpu as pltpu
from jax.sharding import PartitionSpec as P

MESH = pl.DeviceIdType.MESH
VMEM = pltpu.VMEM
DMA = pltpu.SemaphoreType.DMA

decay = 0.9
eps = 1e-06

BLOCK = 1024
COLS = 10
N_F = 16
N_T = 8
RING = 4
ROWS = 64
CHUNKS = 4
CW = BLOCK // CHUNKS
RW = ROWS // CHUNKS
OUT_COLS = 1280
Q = 256

F_STEPS = [(2, 2), (1, 2), (2, 1), (3, 2), (2, 3), (1, 1), (3, 3), (1, 3), (3, 1), (0, 2), (2, 0), (0, 1), (1, 0), (0, 3), (3, 0)]
T_STEPS = [(2, 0), (2, 1), (1, 0), (3, 0), (1, 1), (3, 1), (0, 1)]


def fsdp_at(f, step):
    y = lax.rem(f // RING + step[0], RING)
    x = lax.rem(lax.rem(f, RING) + step[1], RING)
    return y * RING + x


def tp_at(t, step):
    z = lax.rem(t // 2 + step[0], RING)
    return z * 2 + lax.rem(lax.rem(t, 2) + step[1], 2)


def greet(f, t):
    barrier = pltpu.get_barrier_semaphore()
    for step in F_STEPS:
        pl.semaphore_signal(barrier, inc=1, device_id=(fsdp_at(f, step), t), device_id_type=MESH)
    for step in T_STEPS:
        pl.semaphore_signal(barrier, inc=1, device_id=(f, tp_at(t, step)), device_id_type=MESH)
    pl.semaphore_wait(barrier, len(F_STEPS) + len(T_STEPS))


def send(src, dst, send_sem, recv_sem, f, t):
    copy = pltpu.make_async_remote_copy(
        src_ref=src, dst_ref=dst, send_sem=send_sem, recv_sem=recv_sem, device_id=(f, t), device_id_type=MESH
    )
    copy.start()
    return copy


def forward_kernel(owner_ref, g_hbm, o_ref, g_ref, g_sem, s1, r1a, r1b, r1c, r1d, s2, ss1, rs1, ss2, rs2):
    f, t = lax.axis_index("fsdp"), lax.axis_index("tp")
    r1 = (r1a, r1b, r1c, r1d)
    half_row, half = f // 2, lax.rem(f, 2)
    line = half_row * COLS
    owners = [owner_ref[line + c] // N_T for c in range(COLS)]

    def column_of(fsdp):
        col = jnp.int32(0)
        for c in range(COLS):
            col = jnp.where(owners[c] == fsdp, c, col)
        return col

    def piece(col, k):
        return g_ref[col, :, k * CW : (k + 1) * CW]

    loads = []
    for c in range(COLS):
        load = pltpu.make_async_copy(g_hbm.at[:, c * BLOCK : (c + 1) * BLOCK], g_ref.at[c], g_sem.at[c])
        load.start()
        loads.append(load)
    greet(f, t)
    for load in loads:
        load.wait()
    dests = [fsdp_at(f, s) for s in F_STEPS]
    cols = [column_of(d) for d in dests]
    mine = column_of(f)
    sent = []
    for k in range(CHUNKS):
        for i, d in enumerate(dests):
            s1[k, i] = piece(cols[i], k)
            sent.append(send(s1.at[k, i], r1[k].at[half_row, half], ss1.at[k, i], rs1.at[k, i], d, t))
        r1[k][half_row, half] = piece(mine, k)

    def row_of(tp):
        slot = f * N_T + tp

        def body(j, row):
            return jnp.where(owner_ref[j] == slot, j // COLS, row)

        return lax.fori_loop(0, COLS * N_T, body, jnp.int32(0))

    tps = [tp_at(t, s) for s in T_STEPS]
    rows = [row_of(d) for d in tps]
    my_row = row_of(t)
    passed = []
    for k in range(CHUNKS):
        for c in sent[k * len(dests) : (k + 1) * len(dests)]:
            c.wait_recv()
        for i, d in enumerate(tps):
            s2[k, i] = r1[k][rows[i]]
            passed.append(send(s2.at[k, i], o_ref.at[k, :, t], ss2.at[k, i], rs2.at[k, i], f, d))
        o_ref[k, :, t] = r1[k][my_row]
    for c in passed:
        c.wait_recv()
    for c in sent + passed:
        c.wait_send()


def forward(owner, gradient):
    return pl.pallas_call(
        forward_kernel,
        out_shape=jax.ShapeDtypeStruct((CHUNKS, 2, N_T, ROWS, CW), jnp.bfloat16),
        in_specs=[pl.BlockSpec(memory_space=pltpu.SMEM), pl.BlockSpec(memory_space=pl.ANY)],
        out_specs=pl.BlockSpec(memory_space=VMEM),
        scratch_shapes=[VMEM((COLS, ROWS, BLOCK), jnp.bfloat16), DMA((COLS,))]
        + [VMEM((CHUNKS, len(F_STEPS), ROWS, CW), jnp.bfloat16)]
        + [VMEM((N_F // 2, 2, ROWS, CW), jnp.bfloat16)] * CHUNKS
        + [VMEM((CHUNKS, len(T_STEPS), 2, ROWS, CW), jnp.bfloat16)]
        + [DMA((CHUNKS, len(F_STEPS)))] * 2
        + [DMA((CHUNKS, len(T_STEPS)))] * 2,
        compiler_params=pltpu.CompilerParams(collective_id=0, has_side_effects=True, vmem_limit_bytes=32 << 20),
        name="forward",
    )(owner, gradient)


def root_kernel(g_ref, l_ref, r_ref, o_ref, half, full):
    for k in range(CHUNKS):
        g = g_ref[k].reshape(BLOCK, CW)
        for i in range(4):
            rows = pl.ds(i * 256, 256)
            half[rows, k * CW : (k + 1) * CW] = jnp.dot(l_ref[rows], g, preferred_element_type=jnp.float32).astype(jnp.bfloat16)
    total = jnp.zeros((8, 256), jnp.float32)
    for i in range(4):
        rows = pl.ds(i * 256, 256)
        for j in range(4):
            cols = pl.ds(j * 256, 256)
            p = jnp.dot(half[rows], r_ref[:, cols], preferred_element_type=jnp.float32)
            full[rows, cols] = p
            total += jnp.sum((p * p).reshape(32, 8, 256), axis=0)
    factor = lax.rsqrt(jnp.sum(total) / (BLOCK * BLOCK) + eps)
    for i in range(16):
        rows = pl.ds(i * 64, 64)
        o_ref[i // 8, i % 8] = (full[rows] * factor).astype(jnp.bfloat16)


def roots(g, l_root, r_root):
    return pl.pallas_call(
        root_kernel,
        out_shape=jax.ShapeDtypeStruct((2, N_T, ROWS, BLOCK), jnp.bfloat16),
        in_specs=[pl.BlockSpec(memory_space=VMEM)] * 3,
        out_specs=pl.BlockSpec(memory_space=VMEM),
        scratch_shapes=[VMEM((BLOCK, BLOCK), jnp.bfloat16), VMEM((BLOCK, BLOCK), jnp.float32)],
        compiler_params=pltpu.CompilerParams(vmem_limit_bytes=32 << 20),
        name="roots",
    )(g, l_root, r_root)


STAT_ROWS = 128


def stat_kernel(owner_ref, g_ref, l_ref, r_ref, nl_ref, nr_ref):
    i = pl.program_id(0)
    me = lax.axis_index("fsdp") * N_T + lax.axis_index("tp")
    has = lax.fori_loop(0, COLS * N_T, lambda j, n: n + (owner_ref[j] == me).astype(jnp.int32), jnp.int32(0)) > 0
    left = jnp.zeros((STAT_ROWS, BLOCK), jnp.float32)
    for k in range(CHUNKS):
        g = g_ref[k].reshape(BLOCK, CW)
        rows = g_ref[k, i // 4, pl.ds(lax.rem(i, 4) * 2, 2)].reshape(STAT_ROWS, CW)
        left += lax.dot_general(rows, g, (((1,), (1,)), ((), ())), preferred_element_type=jnp.float32)
    nl_ref[...] = decay * l_ref[...] + jnp.where(has, (1.0 - decay) * left, 0.0)
    lane = pl.ds(pl.multiple_of(lax.rem(i, CW // STAT_ROWS) * STAT_ROWS, STAT_ROWS), STAT_ROWS)
    mine = g_ref[i // (CW // STAT_ROWS), :, :, :, lane].reshape(BLOCK, STAT_ROWS)
    for k in range(CHUNKS):
        right = lax.dot_general(
            mine, g_ref[k].reshape(BLOCK, CW), (((0,), (0,)), ((), ())), preferred_element_type=jnp.float32
        )
        cols = slice(k * CW, (k + 1) * CW)
        nr_ref[:, cols] = decay * r_ref[:, cols] + jnp.where(has, (1.0 - decay) * right, 0.0)


def stats(owner, g, l_stat, r_stat):
    block = pl.BlockSpec((STAT_ROWS, BLOCK), lambda i: (i, 0))
    return pl.pallas_call(
        stat_kernel,
        grid=(BLOCK // STAT_ROWS,),
        out_shape=[jax.ShapeDtypeStruct((BLOCK, BLOCK), jnp.float32)] * 2,
        in_specs=[pl.BlockSpec(memory_space=pltpu.SMEM), pl.BlockSpec(memory_space=VMEM), block, block],
        out_specs=[block, block],
        compiler_params=pltpu.CompilerParams(vmem_limit_bytes=32 << 20),
        name="stats",
    )(owner, g, l_stat, r_stat)


def backward_kernel(owner_ref, b_ref, o_ref, ra, rb, rc, rd, s2, xa, xb, xc, xd, s3, ss1, rs1, ss2, rs2, ss3, rs3):
    f, t = lax.axis_index("fsdp"), lax.axis_index("tp")
    r1, r2 = (ra, rb, rc, rd), (xa, xb, xc, xd)
    greet(f, t)
    tps = [tp_at(t, s) for s in T_STEPS]
    dests = [fsdp_at(f, s) for s in F_STEPS]
    n_t, n_f = len(tps), len(dests)
    spread = []
    for k in range(CHUNKS):
        rows = pl.ds(k * RW, RW)
        for i, d in enumerate(tps):
            spread.append(send(b_ref.at[:, d, rows], r1[k].at[t], ss1.at[k, i], rs1.at[k, i], f, d))
        r1[k][t] = b_ref[:, t, rows]

    def tp_of(fsdp):
        line = (fsdp // 2) * COLS
        tp = jnp.int32(0)
        for c in range(COLS):
            o = owner_ref[line + c]
            tp = jnp.where(o // N_T == f, lax.rem(o, N_T), tp)
        return tp

    slots = [tp_of(d) for d in dests]
    my_slot = tp_of(f)
    home = []
    for k in range(CHUNKS):
        for c in spread[k * n_t : (k + 1) * n_t]:
            c.wait_recv()
        for i, d in enumerate(dests):
            piece = r1[k][slots[i], lax.rem(d, 2)]
            for q in range(BLOCK // Q):
                s2[k, i, q] = piece[:, q * Q : (q + 1) * Q]
            home.append(send(s2.at[k, i], r2[k].at[f], ss2.at[k, i], rs2.at[k, i], d, t))
        piece = r1[k][my_slot, lax.rem(f, 2)]
        for q in range(BLOCK // Q):
            r2[k][f, q] = piece[:, q * Q : (q + 1) * Q]

    line = (f // 2) * COLS

    def parts_of(tp):
        parts = []
        for j in range(OUT_COLS // Q):
            chunk = tp * (OUT_COLS // Q) + j
            source = owner_ref[line + chunk // (BLOCK // Q)] // N_T
            parts.append((source, lax.rem(chunk, BLOCK // Q)))
        return parts

    parts = [parts_of(d) for d in tps]
    my_parts = parts_of(t)
    last = []
    for k in range(CHUNKS):
        for c in home[k * n_f : (k + 1) * n_f]:
            c.wait_recv()
        here = pl.ds(pl.multiple_of(t * ROWS + k * RW, RW), RW)
        for i, d in enumerate(tps):
            for j, (source, q) in enumerate(parts[i]):
                s3[k, i, :, j * Q : (j + 1) * Q] = r2[k][source, q]
            last.append(send(s3.at[k, i], o_ref.at[here], ss3.at[k, i], rs3.at[k, i], f, d))
        for j, (source, q) in enumerate(my_parts):
            o_ref[here, j * Q : (j + 1) * Q] = r2[k][source, q]
    for c in last:
        c.wait_recv()
    for c in spread + home + last:
        c.wait_send()


def backward(owner, scaled):
    n_t, n_f = len(T_STEPS), len(F_STEPS)
    return pl.pallas_call(
        backward_kernel,
        out_shape=jax.ShapeDtypeStruct((N_T * ROWS, OUT_COLS), jnp.bfloat16),
        in_specs=[pl.BlockSpec(memory_space=pltpu.SMEM), pl.BlockSpec(memory_space=VMEM)],
        out_specs=pl.BlockSpec(memory_space=VMEM),
        scratch_shapes=[VMEM((N_T, 2, RW, BLOCK), jnp.bfloat16)] * CHUNKS
        + [VMEM((CHUNKS, n_f, BLOCK // Q, RW, Q), jnp.bfloat16)]
        + [VMEM((N_F, BLOCK // Q, RW, Q), jnp.bfloat16)] * CHUNKS
        + [VMEM((CHUNKS, n_t, RW, OUT_COLS), jnp.bfloat16)]
        + [DMA((CHUNKS, n_t))] * 2
        + [DMA((CHUNKS, n_f))] * 2
        + [DMA((CHUNKS, n_t))] * 2,
        compiler_params=pltpu.CompilerParams(collective_id=1, has_side_effects=True, vmem_limit_bytes=32 << 20),
        name="backward",
    )(owner, scaled)


def per_device(gradient, owner, l_stat, r_stat, l_root, r_root):
    g = forward(owner, gradient)
    scaled = roots(g, l_root[0], r_root[0])
    update = backward(owner, scaled)
    new_left, new_right = stats(owner, g, l_stat[0], r_stat[0])
    return (update, new_left[None], new_right[None])


def solution(mesh):
    stat = P(("fsdp", "tp"), None, None)
    return jax.shard_map(
        per_device,
        mesh=mesh,
        in_specs=(P(("fsdp", "tp"), None), P(), stat, stat, stat, stat),
        out_specs=(P("fsdp", "tp"), stat, stat),
        check_vma=False,
    )
```

time: 200 us -> 120 us (0.60)
  Pallas kernels: 0 us -> 115 us
  blocking collectives: 93.9 us -> 0 us
  waiting for transfers between devices: 33.9 us -> 0 us
  matrix products: 33 us -> 0 us
  local copies, waits for them, and re-layouts: 19.9 us -> 4.77 us
  starting transfers between devices: 13.4 us -> 0 us
  other arithmetic: 4.24 us -> 0 us
    pallas_call x0 -> x4, Pallas kernels: none -> 115 us  [the longest x1 47.9 us: backward(): pl.pallas_call(backward_kernel, out_shape=jax.ShapeDtypeStruct((N_T * ROW...]
    all_to_all x3 -> x0, blocking collectives: 93.9 us -> none  [the longest x1 33.7 us: per_device(): lax.all_to_all(forward, 'tp', split_axis=0, concat_axis=3, tiled=True)]
    all_to_all x2 -> x0, waiting for transfers between devices: 33.9 us -> none  [the longest x1 29.8 us: per_device(): lax.all_to_all(outgoing, 'fsdp', split_axis=0, concat_axis=0, tiled=True)]
    dot_general x7 -> x0, matrix products: 33 us -> none  [the longest x1 9.52 us: precondition(): jnp.einsum('sij,sjk->sik', halfway, r_root, preferred_element_type=jnp.fl...]
    all_to_all x2 -> x0, starting transfers between devices: 13.4 us -> none  [the longest x1 7.77 us: per_device(): lax.all_to_all(outgoing, 'fsdp', split_axis=0, concat_axis=0, tiled=True)]
    all_to_all x4 -> x0, local copies, waits for them, and re-layouts: 7.88 us -> none  [the longest x2 4.26 us: per_device(): lax.all_to_all(row_major, 'tp', split_axis=1, concat_axis=0, tiled=True)]
    reshape x5 -> x0, local copies, waits for them, and re-layouts: 7.03 us -> none  [the longest x1 3.56 us: per_device(): pieces = gradient.reshape(shard_rows, column_blocks, block_size)]
    convert_element_type x2 -> x0, local copies, waits for them, and re-layouts: 3.62 us -> none  [the longest x1 2.47 us: per_device(): outgoing = jnp.einsum('fkc,rcb->fkrb', select_rows, pieces, preferred_ele...]
  transfers between devices with their start and end apart: 2 -> 0, of which waited for: 2 -> 0; matrix products, arithmetic and copies ran while one was open for 7% -> 0% of each run, Pallas kernels for 0% -> 0%
where the time goes in v1:
time: 120 us
  Pallas kernels  115 us (96%)
  local copies, waits for them, and re-layouts  4.77 us (4%)
    pallas_call x1, Pallas kernels, backward(): pl.pallas_call(backward_kernel, out_shape=jax.ShapeDtypeStruct((N_T * ROW...  47.9 us
    pallas_call x1, Pallas kernels, forward(): pl.pallas_call(forward_kernel, out_shape=jax.ShapeDtypeStruct((CHUNKS, 2,...  45.9 us
    pallas_call x1, Pallas kernels, stats(): pl.pallas_call(stat_kernel, grid=(BLOCK // STAT_ROWS,), out_shape=[jax.Sh...  15.7 us
    pallas_call x1, Pallas kernels, roots(): pl.pallas_call(root_kernel, out_shape=jax.ShapeDtypeStruct((2, N_T, ROWS,...  5.01 us
    unnamed x15, local copies, waits for them, and re-layouts  4.77 us

profile of v1, /device:TPU:1, one launch (start us, length us, event | category | flops | bytes accessed | tf_op | source)
XLA Modules:
  0.0 120.0 jit_solution(2952236239047494564)
XLA Ops:
  0.6 0.0 copy-start.2
  0.6 0.0 copy-start.4
  0.7 1.5 %copy-done.4 = bf16[64,10240]{1,0:T(8,128)(2,1)S(1)} copy-done((bf16[64,10240]{1,0:T(8,128)(2,1)S(1)}, bf16[64,10240]{1,0:T(8,128)(2,1)}, u32[]{:S(2)}) %copy-start.4) | copy-done | bytes 1310744
  2.1 0.0 copy-start.5
  2.1 0.7 copy-done.5
  2.8 0.0 copy-start.6
  2.8 45.9 %forward.1.g_ref = bf16[4,2,8,64,256]{4,3,2,1,0:T(8,128)(2,1)S(1)} custom-call(s32[80]{0:T(128)S(1)} %copy-done.5, bf16[64,10240]{1,0:T(8,128)(2,1)S(1)} %copy-done.4), custom_call_target="tpu_custom_call" | custom-call | tf_op jit(solution)/shard_map/forward/pallas_call | solution.py:121
  48.7 0.0 copy-done.2
  48.7 0.0 copy-start.3
  48.7 1.6 %copy-done.3 = bf16[1,1024,1024]{2,1,0:T(8,128)(2,1)S(1)} copy-done((bf16[1,1024,1024]{2,1,0:T(8,128)(2,1)S(1)}, bf16[1,1024,1024]{2,1,0:T(8,128)(2,1)}, u32[]{:S(2)}) %copy-start.3) | copy-done | bytes 2097176
  50.3 0.0 copy-start
  50.3 0.0 copy-start.1
  50.3 5.0 %roots.1.b_ref = bf16[2,8,64,1024]{3,2,1,0:T(8,128)(2,1)S(1)} custom-call(bf16[4,2,8,64,256]{4,3,2,1,0:T(8,128)(2,1)S(1)} %forward.1.g_ref, bf16[1024,1024]{1,0:T(8,128)(2,1)S(1)} %bitcast.8, bf16[1024,1024]{1,0:T(8,128)(2,1)S(1)} %bitcast.9), custom_call_target="tpu_custom_call" | custom-call | tf_op jit(solution)/shard_map/roots/pallas_call | solution.py:158
  55.3 0.0 copy-done.6
  55.3 47.9 %backward.1 = bf16[512,1280]{1,0:T(8,128)(2,1)S(1)} custom-call(s32[80]{0:T(128)S(1)} %copy-done.6, bf16[2,8,64,1024]{3,2,1,0:T(8,128)(2,1)S(1)} %roots.1.b_ref), custom_call_target="tpu_custom_call" | custom-call | tf_op jit(solution)/shard_map/backward/pallas_call | solution.py:273
  103.2 0.0 copy-done
  103.2 0.0 copy-done.1
  103.2 15.7 %stats.1 = (f32[1024,1024]{1,0:T(8,128)}, f32[1024,1024]{1,0:T(8,128)}) custom-call(s32[80]{0:T(128)S(1)} %copy-done.6, bf16[4,2,8,64,256]{4,3,2,1,0:T(8,128)(2,1)S(1)} %forward.1.g_ref, f32[1024,1024]{1,0:T(8,128)S(1)} %bitcast.6, f32[1024,1024]{1,0:T(8,128)S(1)} %bitcast.7), custom_call_target="tpu_custom_call" | custom-call | tf_op jit(solution)/shard_map/stats/pallas_call | solution.py:194
  118.9 1.1 copy.10
Async XLA Ops:
  0.6 48.1 %copy-start.2 = (bf16[1,1024,1024]{2,1,0:T(8,128)(2,1)S(1)}, bf16[1,1024,1024]{2,1,0:T(8,128)(2,1)}, u32[]{:S(2)}) copy-start(bf16[1,1024,1024]{2,1,0:T(8,128)(2,1)} %param.10) | copy-start | bytes 6291460
  0.6 1.5 %copy-start.4 = (bf16[64,10240]{1,0:T(8,128)(2,1)S(1)}, bf16[64,10240]{1,0:T(8,128)(2,1)}, u32[]{:S(2)}) copy-start(bf16[64,10240]{1,0:T(8,128)(2,1)} %g_hbm.1) | copy-start | bytes 3932164
  2.1 0.7 copy-start.5
  2.8 52.6 %copy-start.6 = (s32[80]{0:T(128)S(1)}, s32[80]{0:T(128)}, u32[]{:S(2)}) copy-start(s32[80]{0:T(128)} %owner_ref.5) | copy-start | bytes 964
  48.7 1.6 %copy-start.3 = (bf16[1,1024,1024]{2,1,0:T(8,128)(2,1)S(1)}, bf16[1,1024,1024]{2,1,0:T(8,128)(2,1)}, u32[]{:S(2)}) copy-start(bf16[1,1024,1024]{2,1,0:T(8,128)(2,1)} %param.11) | copy-start | bytes 6291460
  50.3 52.9 %copy-start = (f32[1,1024,1024]{2,1,0:T(8,128)S(1)}, f32[1,1024,1024]{2,1,0:T(8,128)}, u32[]{:S(2)}) copy-start(f32[1,1024,1024]{2,1,0:T(8,128)} %param.8) | copy-start | bytes 12582916
  50.3 52.9 %copy-start.1 = (f32[1,1024,1024]{2,1,0:T(8,128)S(1)}, f32[1,1024,1024]{2,1,0:T(8,128)}, u32[]{:S(2)}) copy-start(f32[1,1024,1024]{2,1,0:T(8,128)} %param.9) | copy-start | bytes 12582916

commit v2 on v0

v2 whole, which is shorter than its diff:
```python
import jax
import jax.numpy as jnp
from jax import lax
from jax.experimental import pallas as pl
from jax.experimental.pallas import tpu as pltpu
from jax.sharding import PartitionSpec as P

MESH = pl.DeviceIdType.MESH
VMEM = pltpu.VMEM
DMA = pltpu.SemaphoreType.DMA
f32, bf16 = jnp.float32, jnp.bfloat16

decay = 0.9
eps = 1e-06

BLOCK = 1024
LINES = 8
COLS = 10
N_F = 16
N_T = 8
RING = 4
ROWS = 64
CW = 128
FWD = BLOCK // CW
PAIR = 256
RW = 16
GROUPS = ROWS // RW
HW = 512
HALVES = BLOCK // HW
BWD = GROUPS * HALVES
OUT_COLS = 1280
Q = 256
QH = HW // Q
TILE = 256

F_STEPS = [(2, 2), (1, 2), (2, 1), (3, 2), (2, 3), (1, 1), (3, 3), (1, 3), (3, 1), (0, 2), (2, 0), (0, 1), (1, 0), (0, 3), (3, 0)]
T_STEPS = [(2, 0), (2, 1), (1, 0), (3, 0), (1, 1), (3, 1), (0, 1)]
NF, NT = len(F_STEPS), len(T_STEPS)


def fsdp_at(f, step):
    y = (f // RING + step[0]) % RING
    x = (f % RING + step[1]) % RING
    return y * RING + x


def tp_at(t, step):
    return ((t // 2 + step[0]) % RING) * 2 + (t % 2 + step[1]) % 2


def send(src, dst, send_sem, recv_sem, f, t):
    pltpu.make_async_remote_copy(
        src_ref=src, dst_ref=dst, send_sem=send_sem, recv_sem=recv_sem, device_id=(f, t), device_id_type=MESH
    ).start()


def drain(like, sem):
    pltpu.make_async_copy(like, like, sem).wait()


def rows_of(ref, i):
    return ref[i // 2, pl.ds((i % 2) * 4, 4)].reshape(TILE, ref.shape[-1])


def kernel(owner_ref, g_hbm, ls_hbm, rs_hbm, lr_hbm, rr_hbm, upd, nl, nr, *scratch):
    (gv, lr, rr, g, gt, full, s, s1, s2, b2, b3, slots) = scratch[:12]
    r1 = scratch[12 : 12 + FWD]
    ra = scratch[12 + FWD : 12 + FWD + BWD]
    rx = scratch[12 + FWD + BWD : 12 + FWD + BWD + GROUPS]
    (gsem, lsem, ss1, rs1, ss2, rs2, sa, ra_sem, sx, rx_sem, sz, rz_sem) = scratch[12 + FWD + BWD + GROUPS :]

    f, t = lax.axis_index("fsdp"), lax.axis_index("tp")
    line, part = f // 2, f % 2
    fs = [fsdp_at(f, step) for step in F_STEPS]
    ts = [tp_at(t, step) for step in T_STEPS]

    loads = [pltpu.make_async_copy(g_hbm.at[:, c * BLOCK : (c + 1) * BLOCK], gv.at[c], gsem.at[c]) for c in range(COLS)]
    big = [
        pltpu.make_async_copy(lr_hbm, lr, lsem.at[0]),
        pltpu.make_async_copy(rr_hbm, rr, lsem.at[1]),
        pltpu.make_async_copy(ls_hbm, nl, lsem.at[2]),
        pltpu.make_async_copy(rs_hbm, nr, lsem.at[3]),
    ]
    for load in loads + big:
        load.start()

    barrier = pltpu.get_barrier_semaphore()
    for d in fs:
        pl.semaphore_signal(barrier, inc=1, device_id=(d, t), device_id_type=MESH)
    for d in ts:
        pl.semaphore_signal(barrier, inc=1, device_id=(f, d), device_id_type=MESH)

    near = [owner_ref[line * COLS + c] >> 3 for c in range(COLS)]

    def column_of(fsdp):
        col = jnp.int32(0)
        for c in range(COLS):
            col = jnp.where(near[c] == fsdp, c, col)
        return col

    cols = [column_of(d) for d in fs]
    my_col = column_of(f)
    pl.semaphore_wait(barrier, NF + NT)
    for load in loads:
        load.wait()

    for k in range(FWD):
        cut = slice(k * CW, (k + 1) * CW)
        for i, d in enumerate(fs):
            s1[k, i] = gv[cols[i], :, cut]
            send(s1.at[k, i], r1[k].at[line, part], ss1.at[k], rs1.at[k], d, t)
        r1[k][line, part] = gv[my_col, :, cut]

    owned = [jnp.int32(-1)] * N_T
    for r in range(LINES):
        tp = jnp.int32(0)
        for c in range(COLS):
            o = owner_ref[r * COLS + c]
            here = (o >> 3) == f
            low = o & 7
            tp = jnp.where(here, low, tp)
            away = jnp.where(here, low, -1)
            owned = [jnp.where(away == p, r, owned[p]) for p in range(N_T)]
        slots[N_T + r] = tp
    for p in range(N_T):
        slots[p] = owned[p]
    mine = slots[t]
    has = mine >= 0
    lines = [jnp.maximum(slots[d], 0) for d in ts]
    my_line = jnp.maximum(mine, 0)

    def products(m, total):
        pair = slice(m * PAIR, (m + 1) * PAIR)
        drain(s2.at[2 * m], rs2.at[2 * m])
        drain(s2.at[2 * m + 1], rs2.at[2 * m + 1])
        block = g[:, :, :, pair].reshape(BLOCK, PAIR)

        def step(i, total):
            rows = pl.ds(pl.multiple_of(i * TILE, TILE), TILE)
            h = jnp.dot(lr[rows], block, preferred_element_type=f32).astype(bf16)
            for j in range(BLOCK // TILE):
                cut = slice(j * TILE, (j + 1) * TILE)
                p = jnp.dot(h, rr[pair, cut], preferred_element_type=f32)
                if m:
                    p += full[rows, cut]
                full[rows, cut] = p
                if m == BLOCK // PAIR - 1:
                    total += jnp.sum((p * p).reshape(TILE // 8, 8, TILE), axis=0)
            return total

        total = lax.fori_loop(0, BLOCK // TILE, step, total)
        gt[pair, :] = block.T
        return total

    total = jnp.zeros((8, TILE), f32)
    for k in range(FWD):
        drain(s1.at[k], rs1.at[k])
        cut = slice(k * CW, (k + 1) * CW)
        for i, d in enumerate(ts):
            s2[k, i] = r1[k][lines[i]]
            send(s2.at[k, i], g.at[:, t, :, cut], ss2.at[k], rs2.at[k], f, d)
        g[:, t, :, cut] = r1[k][my_line]
        if k == 3:
            for load in big[:2]:
                load.wait()
            total = products(0, total)
        elif k in (5, 7):
            total = products((k - 3) // 2, total)
    total = products(BLOCK // PAIR - 1, total)
    factor = lax.rsqrt(jnp.sum(total) / (BLOCK * BLOCK) + eps)

    for r in range(GROUPS):
        for h in range(2):
            for p in range(N_T):
                start = h * (BLOCK // 2) + p * ROWS + r * RW
                s[h, p, r * RW : (r + 1) * RW] = (full[start : start + RW] * factor).astype(bf16)
        rows = pl.ds(r * RW, RW)
        for e in range(HALVES):
            c = r * HALVES + e
            cut = pl.ds(e * HW, HW)
            for i, d in enumerate(ts):
                send(s.at[:, d, rows, cut], ra[c].at[t], sa.at[c], ra_sem.at[c], f, d)
            ra[c][t] = s[:, t, rows, cut]

    def left(i):
        rows = pl.ds(i * TILE, TILE)
        a = rows_of(g, i)
        for j in range(BLOCK // TILE):
            cut = slice(j * TILE, (j + 1) * TILE)
            p = jnp.dot(a, gt[:, cut], preferred_element_type=f32)
            nl[rows, cut] = decay * nl[rows, cut] + jnp.where(has, (1.0 - decay) * p, 0.0)

    def right(i):
        rows = pl.ds(i * TILE, TILE)
        a = gt[rows]
        for j in range(BLOCK // TILE):
            cut = slice(j * TILE, (j + 1) * TILE)
            p = jnp.dot(a, g[:, :, :, cut].reshape(BLOCK, TILE), preferred_element_type=f32)
            nr[rows, cut] = decay * nr[rows, cut] + jnp.where(has, (1.0 - decay) * p, 0.0)

    for load in big[2:]:
        load.wait()
    work = [lambda i=i: left(i) for i in range(4)] + [lambda i=i: right(i) for i in range(4)]
    work.pop(0)()
    work.pop(0)()

    def parts_of(tp):
        parts = []
        for j in range(OUT_COLS // Q):
            chunk = tp * (OUT_COLS // Q) + j
            parts.append((owner_ref[line * COLS + chunk // (BLOCK // Q)] >> 3, chunk % (BLOCK // Q)))
        return parts

    sources = [slots[N_T + d // 2] for d in fs]
    my_source = slots[N_T + line]
    parts = [parts_of(d) for d in ts]
    my_parts = parts_of(t)

    def finish(r):
        for e in range(HALVES):
            drain(b2.at[r * HALVES + e], rx_sem.at[r * HALVES + e])
        here = pl.ds(pl.multiple_of(t * ROWS + r * RW, RW), RW)
        for i, d in enumerate(ts):
            for j, (source, q) in enumerate(parts[i]):
                b3[r, i, :, j * Q : (j + 1) * Q] = rx[r][source, q]
            send(b3.at[r, i], upd.at[here], sz.at[r], rz_sem.at[r], f, d)
        for j, (source, q) in enumerate(my_parts):
            upd[here, j * Q : (j + 1) * Q] = rx[r][source, q]

    for c in range(BWD):
        r, e = c // HALVES, c % HALVES
        drain(ra[c].at[pl.ds(0, NT)], ra_sem.at[c])
        for i, d in enumerate(fs):
            piece = ra[c][sources[i], d % 2]
            for q in range(QH):
                b2[c, i, q] = piece[:, q * Q : (q + 1) * Q]
            send(b2.at[c, i], rx[r].at[f, pl.ds(e * QH, QH)], sx.at[c], rx_sem.at[c], d, t)
        piece = ra[c][my_source, part]
        for q in range(QH):
            rx[r][f, e * QH + q] = piece[:, q * Q : (q + 1) * Q]
        if e == HALVES - 1 and r > 0:
            finish(r - 1)
        if work:
            work.pop(0)()
    finish(GROUPS - 1)

    for k in range(FWD):
        drain(s1.at[k], ss1.at[k])
        drain(s2.at[k], ss2.at[k])
    for c in range(BWD):
        drain(ra[c].at[pl.ds(0, NT)], sa.at[c])
        drain(b2.at[c], sx.at[c])
    for r in range(GROUPS):
        drain(b3.at[r], sz.at[r])
        drain(b3.at[r], rz_sem.at[r])


def step(owner, gradient, l_stat, r_stat, l_root, r_root):
    hbm = pl.BlockSpec(memory_space=pltpu.HBM)
    vmem = pl.BlockSpec(memory_space=VMEM)
    return pl.pallas_call(
        kernel,
        out_shape=[
            VMEM((N_T * ROWS, OUT_COLS), bf16),
            VMEM((BLOCK, BLOCK), f32),
            VMEM((BLOCK, BLOCK), f32),
        ],
        in_specs=[pl.BlockSpec(memory_space=pltpu.SMEM)] + [hbm] * 5,
        out_specs=[vmem] * 3,
        scratch_shapes=[
            VMEM((COLS, ROWS, BLOCK), bf16),
            VMEM((BLOCK, BLOCK), bf16),
            VMEM((BLOCK, BLOCK), bf16),
            VMEM((2, N_T, ROWS, BLOCK), bf16),
            VMEM((BLOCK, BLOCK), bf16),
            VMEM((BLOCK, BLOCK), f32),
            VMEM((2, N_T, ROWS, BLOCK), bf16),
            VMEM((FWD, NF, ROWS, CW), bf16),
            VMEM((FWD, NT, 2, ROWS, CW), bf16),
            VMEM((BWD, NF, QH, RW, Q), bf16),
            VMEM((GROUPS, NT, RW, OUT_COLS), bf16),
            pltpu.SMEM((N_T + LINES,), jnp.int32),
        ]
        + [VMEM((LINES, 2, ROWS, CW), bf16)] * FWD
        + [VMEM((N_T, 2, RW, HW), bf16)] * BWD
        + [VMEM((N_F, BLOCK // Q, RW, Q), bf16)] * GROUPS
        + [DMA((COLS,)), DMA((4,))]
        + [DMA((FWD,))] * 4
        + [DMA((BWD,))] * 4
        + [DMA((GROUPS,))] * 2,
        compiler_params=pltpu.CompilerParams(collective_id=0, has_side_effects=True, vmem_limit_bytes=40 << 20),
        name="shampoo",
    )(owner, gradient, l_stat, r_stat, l_root, r_root)


def write_kernel(a, b, c, oa, ob, oc, sems):
    copies = [pltpu.make_async_copy(x, y, sems.at[i]) for i, (x, y) in enumerate([(a, oa), (b, ob), (c, oc)])]
    for copy in copies:
        copy.start()
    for copy in copies:
        copy.wait()


def write(update, new_left, new_right):
    outs = (update, new_left, new_right)
    return pl.pallas_call(
        write_kernel,
        out_shape=[jax.ShapeDtypeStruct(x.shape, x.dtype) for x in outs],
        in_specs=[pl.BlockSpec(memory_space=VMEM)] * 3,
        out_specs=[pl.BlockSpec(memory_space=pltpu.HBM)] * 3,
        scratch_shapes=[DMA((3,))],
        compiler_params=pltpu.CompilerParams(vmem_limit_bytes=16 << 20),
        name="write",
    )(*outs)


def per_device(gradient, owner, l_stat, r_stat, l_root, r_root):
    args = [pltpu.with_memory_space_constraint(x, pltpu.HBM) for x in (gradient, l_stat[0], r_stat[0], l_root[0], r_root[0])]
    update, new_left, new_right = write(*step(owner, *args))
    return (update, new_left[None], new_right[None])


def solution(mesh):
    stat = P(("fsdp", "tp"), None, None)
    return jax.shard_map(
        per_device,
        mesh=mesh,
        in_specs=(P(("fsdp", "tp"), None), P(), stat, stat, stat, stat),
        out_specs=(P("fsdp", "tp"), stat, stat),
        check_vma=False,
    )
```

time: 200 us -> 88.5 us (0.44)
  blocking collectives: 93.9 us -> 0 us
  Pallas kernels: 0 us -> 87 us
  waiting for transfers between devices: 33.9 us -> 0 us
  matrix products: 33 us -> 0 us
  local copies, waits for them, and re-layouts: 19.9 us -> 0.65 us
  starting transfers between devices: 13.4 us -> 0 us
  other arithmetic: 4.24 us -> 0 us
    all_to_all x3 -> x0, blocking collectives: 93.9 us -> none  [the longest x1 33.7 us: per_device(): lax.all_to_all(forward, 'tp', split_axis=0, concat_axis=3, tiled=True)]
    pallas_call x0 -> x2, Pallas kernels: none -> 87 us  [the longest x1 83.1 us: step(): pl.pallas_call(kernel, out_shape=[VMEM((N_T * ROWS, OUT_COLS), bf16), VME...]
    all_to_all x2 -> x0, waiting for transfers between devices: 33.9 us -> none  [the longest x1 29.8 us: per_device(): lax.all_to_all(outgoing, 'fsdp', split_axis=0, concat_axis=0, tiled=True)]
    dot_general x7 -> x0, matrix products: 33 us -> none  [the longest x1 9.52 us: precondition(): jnp.einsum('sij,sjk->sik', halfway, r_root, preferred_element_type=jnp.fl...]
    all_to_all x2 -> x0, starting transfers between devices: 13.4 us -> none  [the longest x1 7.77 us: per_device(): lax.all_to_all(outgoing, 'fsdp', split_axis=0, concat_axis=0, tiled=True)]
    all_to_all x4 -> x0, local copies, waits for them, and re-layouts: 7.88 us -> none  [the longest x2 4.26 us: per_device(): lax.all_to_all(row_major, 'tp', split_axis=1, concat_axis=0, tiled=True)]
    reshape x5 -> x0, local copies, waits for them, and re-layouts: 7.03 us -> none  [the longest x1 3.56 us: per_device(): pieces = gradient.reshape(shard_rows, column_blocks, block_size)]
    convert_element_type x2 -> x0, local copies, waits for them, and re-layouts: 3.62 us -> none  [the longest x1 2.47 us: per_device(): outgoing = jnp.einsum('fkc,rcb->fkrb', select_rows, pieces, preferred_ele...]
  transfers between devices with their start and end apart: 2 -> 0, of which waited for: 2 -> 0; matrix products, arithmetic and copies ran while one was open for 7% -> 0% of each run, Pallas kernels for 0% -> 0%
where the time goes in v2:
time: 88.5 us; the launch traced here: 88.3 us
  Pallas kernels  87 us (98%)
    pallas_call x1, Pallas kernels, step(): pl.pallas_call(kernel, out_shape=[VMEM((N_T * ROWS, OUT_COLS), bf16), VME...  83.1 us
    pallas_call x1, Pallas kernels, write(): pl.pallas_call(write_kernel, out_shape=[jax.ShapeDtypeStruct(x.shape, x.d...  3.85 us

profile of v2, /device:TPU:1, one launch (start us, length us, event | category | flops | bytes accessed | tf_op | source)
XLA Modules:
  0.0 88.3 jit_solution(6725312186343536848)
XLA Ops:
  0.6 0.0 copy-start
  0.6 0.6 copy-done
  1.3 83.1 %shampoo.1 = (bf16[512,1280]{1,0:T(8,128)(2,1)S(1)}, f32[1024,1024]{1,0:T(8,128)S(1)}, f32[1024,1024]{1,0:T(8,128)S(1)}) custom-call(s32[80]{0:T(128)S(1)} %copy-done, bf16[64,10240]{1,0:T(8,128)(2,1)} %g_hbm.1, f32[1024,1024]{1,0:T(8,128)} %bitcast.6, f32[1024,1024]{1,0:T(8,128)} %bitcast.7, bf16[1024,1024]{1,0:T(8,128)(2,1)} %bitcast.8, ...), custom_call_target="tpu_custom_call" | custom-call | tf_op jit(solution)/shard_map/shampoo/pallas_call | solution.py:261
  84.4 3.9 %write.1 = (bf16[512,1280]{1,0:T(8,128)(2,1)}, f32[1024,1024]{1,0:T(8,128)}, f32[1024,1024]{1,0:T(8,128)}) custom-call(bf16[512,1280]{1,0:T(8,128)(2,1)S(1)} %get-tuple-element.9.a, f32[1024,1024]{1,0:T(8,128)S(1)} %get-tuple-element.10.b, f32[1024,1024]{1,0:T(8,128)S(1)} %get-tuple-element.11.c), custom_call_target="tpu_custom_call" | custom-call | tf_op jit(solution)/shard_map/write/pallas_call | solution.py:306
Async XLA Ops:
  0.6 0.7 copy-start

commit v3 on v2

--- a/solution.py
+++ b/solution.py
@@ -21,7 +21,10 @@
 RING = 4
 ROWS = 64
 CW = 128
-FWD = BLOCK // CW
+CHUNKS = [(0, 0, 32), (0, 32, 32)]
+CHUNKS += [(c, 0, 64) for c in range(CW, BLOCK - CW, CW)]
+CHUNKS += [(BLOCK - CW, 0, 32), (BLOCK - CW, 32, 32)]
+FWD = len(CHUNKS)
 PAIR = 256
 RW = 16
 GROUPS = ROWS // RW
@@ -62,18 +65,30 @@
     return ref[i // 2, pl.ds((i % 2) * 4, 4)].reshape(TILE, ref.shape[-1])
 
 
-def kernel(owner_ref, g_hbm, ls_hbm, rs_hbm, lr_hbm, rr_hbm, upd, nl, nr, *scratch):
-    (gv, lr, rr, g, gt, full, s, s1, s2, b2, b3, slots) = scratch[:12]
-    r1 = scratch[12 : 12 + FWD]
-    ra = scratch[12 + FWD : 12 + FWD + BWD]
-    rx = scratch[12 + FWD + BWD : 12 + FWD + BWD + GROUPS]
-    (gsem, lsem, ss1, rs1, ss2, rs2, sa, ra_sem, sx, rx_sem, sz, rz_sem) = scratch[12 + FWD + BWD + GROUPS :]
+def kernel(owner_hbm, g_hbm, ls_hbm, rs_hbm, lr_hbm, rr_hbm, upd, nl, nr, *scratch):
+    scratch = list(scratch)
+
+    def take(n):
+        taken, scratch[:n] = scratch[:n], []
+        return taken
+
+    gv, lr, rr, g, gt, full, s, b2, b3, owner_ref, slots = take(11)
+    s1, s2, r1, ra, rx = take(FWD), take(FWD), take(FWD), take(BWD), take(GROUPS)
+    gsem, lsem, ss1, rs1, ss2, rs2, sa, ra_sem, sx, rx_sem, sz, rz_sem = scratch
 
     f, t = lax.axis_index("fsdp"), lax.axis_index("tp")
     line, part = f // 2, f % 2
     fs = [fsdp_at(f, step) for step in F_STEPS]
     ts = [tp_at(t, step) for step in T_STEPS]
 
+    barrier = pltpu.get_barrier_semaphore()
+    for d in fs:
+        pl.semaphore_signal(barrier, inc=1, device_id=(d, t), device_id_type=MESH)
+    for d in ts:
+        pl.semaphore_signal(barrier, inc=1, device_id=(f, d), device_id_type=MESH)
+
+    names = pltpu.make_async_copy(owner_hbm, owner_ref, lsem.at[4])
+    names.start()
     loads = [pltpu.make_async_copy(g_hbm.at[:, c * BLOCK : (c + 1) * BLOCK], gv.at[c], gsem.at[c]) for c in range(COLS)]
     big = [
         pltpu.make_async_copy(lr_hbm, lr, lsem.at[0]),
@@ -81,14 +96,9 @@
         pltpu.make_async_copy(ls_hbm, nl, lsem.at[2]),
         pltpu.make_async_copy(rs_hbm, nr, lsem.at[3]),
     ]
-    for load in loads + big:
+    for load in loads:
         load.start()
-
-    barrier = pltpu.get_barrier_semaphore()
-    for d in fs:
-        pl.semaphore_signal(barrier, inc=1, device_id=(d, t), device_id_type=MESH)
-    for d in ts:
-        pl.semaphore_signal(barrier, inc=1, device_id=(f, d), device_id_type=MESH)
+    names.wait()
 
     near = [owner_ref[line * COLS + c] >> 3 for c in range(COLS)]
 
@@ -104,12 +114,14 @@
     for load in loads:
         load.wait()
 
-    for k in range(FWD):
-        cut = slice(k * CW, (k + 1) * CW)
+    for k, (c0, r0, n) in enumerate(CHUNKS):
         for i, d in enumerate(fs):
-            s1[k, i] = gv[cols[i], :, cut]
-            send(s1.at[k, i], r1[k].at[line, part], ss1.at[k], rs1.at[k], d, t)
-        r1[k][line, part] = gv[my_col, :, cut]
+            s1[k][i] = gv[cols[i], r0 : r0 + n, c0 : c0 + CW]
+            send(s1[k].at[i], r1[k].at[line, part], ss1.at[k], rs1.at[k], d, t)
+        r1[k][line, part] = gv[my_col, r0 : r0 + n, c0 : c0 + CW]
+        if k == 1:
+            for load in big:
+                load.start()
 
     owned = [jnp.int32(-1)] * N_T
     for r in range(LINES):
@@ -129,44 +141,41 @@
     lines = [jnp.maximum(slots[d], 0) for d in ts]
     my_line = jnp.maximum(mine, 0)
 
-    def products(m, total):
+    def turn(m):
         pair = slice(m * PAIR, (m + 1) * PAIR)
-        drain(s2.at[2 * m], rs2.at[2 * m])
-        drain(s2.at[2 * m + 1], rs2.at[2 * m + 1])
-        block = g[:, :, :, pair].reshape(BLOCK, PAIR)
-
-        def step(i, total):
-            rows = pl.ds(pl.multiple_of(i * TILE, TILE), TILE)
-            h = jnp.dot(lr[rows], block, preferred_element_type=f32).astype(bf16)
+        gt[pair, :] = g[:, :, :, pair].reshape(BLOCK, PAIR).T
+
+    def products(m):
+        pair = slice(m * PAIR, (m + 1) * PAIR)
+        for k, (c0, _, _) in enumerate(CHUNKS):
+            if c0 // PAIR == m:
+                drain(s2[k], rs2.at[k])
+        h = jnp.dot(lr[...], g[:, :, :, pair].reshape(BLOCK, PAIR), preferred_element_type=f32).astype(bf16)
+        total = jnp.zeros((8, TILE), f32)
+        for i in range(BLOCK // TILE):
+            rows = slice(i * TILE, (i + 1) * TILE)
             for j in range(BLOCK // TILE):
                 cut = slice(j * TILE, (j + 1) * TILE)
-                p = jnp.dot(h, rr[pair, cut], preferred_element_type=f32)
+                p = jnp.dot(h[rows], rr[pair, cut], preferred_element_type=f32)
                 if m:
                     p += full[rows, cut]
                 full[rows, cut] = p
-                if m == BLOCK // PAIR - 1:
-                    total += jnp.sum((p * p).reshape(TILE // 8, 8, TILE), axis=0)
-            return total
-
-        total = lax.fori_loop(0, BLOCK // TILE, step, total)
-        gt[pair, :] = block.T
+                total += jnp.sum((p * p).reshape(TILE // 8, 8, TILE), axis=0)
         return total
 
-    total = jnp.zeros((8, TILE), f32)
-    for k in range(FWD):
-        drain(s1.at[k], rs1.at[k])
-        cut = slice(k * CW, (k + 1) * CW)
+    for k, (c0, r0, n) in enumerate(CHUNKS):
+        drain(s1[k], rs1.at[k])
         for i, d in enumerate(ts):
-            s2[k, i] = r1[k][lines[i]]
-            send(s2.at[k, i], g.at[:, t, :, cut], ss2.at[k], rs2.at[k], f, d)
-        g[:, t, :, cut] = r1[k][my_line]
-        if k == 3:
+            s2[k][i] = r1[k][lines[i]]
+            send(s2[k].at[i], g.at[:, t, pl.ds(r0, n), c0 : c0 + CW], ss2.at[k], rs2.at[k], f, d)
+        g[:, t, r0 : r0 + n, c0 : c0 + CW] = r1[k][my_line]
+        if k == 4:
             for load in big[:2]:
                 load.wait()
-            total = products(0, total)
-        elif k in (5, 7):
-            total = products((k - 3) // 2, total)
-    total = products(BLOCK // PAIR - 1, total)
+        if k in (5, 7, 9):
+            products((k - 5) // 2)
+            turn((k - 5) // 2)
+    total = products(BLOCK // PAIR - 1)
     factor = lax.rsqrt(jnp.sum(total) / (BLOCK * BLOCK) + eps)
 
     for r in range(GROUPS):
@@ -198,6 +207,7 @@
             p = jnp.dot(a, g[:, :, :, cut].reshape(BLOCK, TILE), preferred_element_type=f32)
             nr[rows, cut] = decay * nr[rows, cut] + jnp.where(has, (1.0 - decay) * p, 0.0)
 
+    turn(BLOCK // PAIR - 1)
     for load in big[2:]:
         load.wait()
     work = [lambda i=i: left(i) for i in range(4)] + [lambda i=i: right(i) for i in range(4)]
@@ -245,8 +255,8 @@
     finish(GROUPS - 1)
 
     for k in range(FWD):
-        drain(s1.at[k], ss1.at[k])
-        drain(s2.at[k], ss2.at[k])
+        drain(s1[k], ss1.at[k])
+        drain(s2[k], ss2.at[k])
     for c in range(BWD):
         drain(ra[c].at[pl.ds(0, NT)], sa.at[c])
         drain(b2.at[c], sx.at[c])
@@ -265,7 +275,7 @@
             VMEM((BLOCK, BLOCK), f32),
             VMEM((BLOCK, BLOCK), f32),
         ],
-        in_specs=[pl.BlockSpec(memory_space=pltpu.SMEM)] + [hbm] * 5,
+        in_specs=[hbm] * 6,
         out_specs=[vmem] * 3,
         scratch_shapes=[
             VMEM((COLS, ROWS, BLOCK), bf16),
@@ -275,16 +285,17 @@
             VMEM((BLOCK, BLOCK), bf16),
             VMEM((BLOCK, BLOCK), f32),
             VMEM((2, N_T, ROWS, BLOCK), bf16),
-            VMEM((FWD, NF, ROWS, CW), bf16),
-            VMEM((FWD, NT, 2, ROWS, CW), bf16),
             VMEM((BWD, NF, QH, RW, Q), bf16),
             VMEM((GROUPS, NT, RW, OUT_COLS), bf16),
+            pltpu.SMEM((LINES * COLS,), jnp.int32),
             pltpu.SMEM((N_T + LINES,), jnp.int32),
         ]
-        + [VMEM((LINES, 2, ROWS, CW), bf16)] * FWD
+        + [VMEM((NF, n, CW), bf16) for _, _, n in CHUNKS]
+        + [VMEM((NT, 2, n, CW), bf16) for _, _, n in CHUNKS]
+        + [VMEM((LINES, 2, n, CW), bf16) for _, _, n in CHUNKS]
         + [VMEM((N_T, 2, RW, HW), bf16)] * BWD
         + [VMEM((N_F, BLOCK // Q, RW, Q), bf16)] * GROUPS
-        + [DMA((COLS,)), DMA((4,))]
+        + [DMA((COLS,)), DMA((5,))]
         + [DMA((FWD,))] * 4
         + [DMA((BWD,))] * 4
         + [DMA((GROUPS,))] * 2,
@@ -315,8 +326,8 @@
 
 
 def per_device(gradient, owner, l_stat, r_stat, l_root, r_root):
-    args = [pltpu.with_memory_space_constraint(x, pltpu.HBM) for x in (gradient, l_stat[0], r_stat[0], l_root[0], r_root[0])]
-    update, new_left, new_right = write(*step(owner, *args))
+    args = [pltpu.with_memory_space_constraint(x, pltpu.HBM) for x in (owner, gradient, l_stat[0], r_stat[0], l_root[0], r_root[0])]
+    update, new_left, new_right = write(*step(*args))
     return (update, new_left[None], new_right[None])
 
 

time: 88.5 us -> 85.4 us (0.965)
  Pallas kernels: 87 us -> 84.4 us
    pallas_call x1, Pallas kernels: 83.1 us -> 80.6 us  [step(): pl.pallas_call(kernel, out_shape=[VMEM((N_T * ROWS, OUT_COLS), bf16), VME...]
where the time goes in v3:
time: 85.4 us; the launch traced here: 85.2 us
  Pallas kernels  84.4 us (99%)
    pallas_call x1, Pallas kernels, step(): pl.pallas_call(kernel, out_shape=[VMEM((N_T * ROWS, OUT_COLS), bf16), VME...  80.6 us
    pallas_call x1, Pallas kernels, write(): pl.pallas_call(write_kernel, out_shape=[jax.ShapeDtypeStruct(x.shape, x.d...  3.85 us

profile of v3, /device:TPU:1, one launch (start us, length us, event | category | flops | bytes accessed | tf_op | source)
XLA Modules:
  0.0 85.2 jit_solution(12666462025517707723)
XLA Ops:
  0.6 80.6 %shampoo.1 = (bf16[512,1280]{1,0:T(8,128)(2,1)S(1)}, f32[1024,1024]{1,0:T(8,128)S(1)}, f32[1024,1024]{1,0:T(8,128)S(1)}) custom-call(s32[80]{0:T(128)} %owner_hbm.1, bf16[64,10240]{1,0:T(8,128)(2,1)} %g_hbm.1, f32[1024,1024]{1,0:T(8,128)} %bitcast.6, f32[1024,1024]{1,0:T(8,128)} %bitcast.7, bf16[1024,1024]{1,0:T(8,128)(2,1)} %bitcast.8, ...), custom_call_target="tpu_custom_call" | custom-call | tf_op jit(solution)/shard_map/shampoo/pallas_call | solution.py:271
  81.2 3.9 %write.1 = (bf16[512,1280]{1,0:T(8,128)(2,1)}, f32[1024,1024]{1,0:T(8,128)}, f32[1024,1024]{1,0:T(8,128)}) custom-call(bf16[512,1280]{1,0:T(8,128)(2,1)S(1)} %get-tuple-element.9.a, f32[1024,1024]{1,0:T(8,128)S(1)} %get-tuple-element.10.b, f32[1024,1024]{1,0:T(8,128)S(1)} %get-tuple-element.11.c), custom_call_target="tpu_custom_call" | custom-call | tf_op jit(solution)/shard_map/write/pallas_call | solution.py:317

commit v4 on v3

--- a/solution.py
+++ b/solution.py
@@ -28,13 +28,11 @@
 PAIR = 256
 RW = 16
 GROUPS = ROWS // RW
-HW = 512
-HALVES = BLOCK // HW
-BWD = GROUPS * HALVES
 OUT_COLS = 1280
 Q = 256
-QH = HW // Q
 TILE = 256
+BACK = [(0, 0, 512), (0, 512, 512)] + [(r, c, 512) for r in range(1, GROUPS) for c in (0, 512)]
+BWD = len(BACK)
 
 F_STEPS = [(2, 2), (1, 2), (2, 1), (3, 2), (2, 3), (1, 1), (3, 3), (1, 3), (3, 1), (0, 2), (2, 0), (0, 1), (1, 0), (0, 3), (3, 0)]
 T_STEPS = [(2, 0), (2, 1), (1, 0), (3, 0), (1, 1), (3, 1), (0, 1)]
@@ -72,9 +70,9 @@
         taken, scratch[:n] = scratch[:n], []
         return taken
 
-    gv, lr, rr, g, gt, full, s, b2, b3, owner_ref, slots = take(11)
-    s1, s2, r1, ra, rx = take(FWD), take(FWD), take(FWD), take(BWD), take(GROUPS)
-    gsem, lsem, ss1, rs1, ss2, rs2, sa, ra_sem, sx, rx_sem, sz, rz_sem = scratch
+    gv, lr, rr, g, gt, full, s, b3, fac, fac_out, owner_ref, slots = take(12)
+    s1, s2, r1, ra, b2, rx = take(FWD), take(FWD), take(FWD), take(BWD), take(BWD), take(GROUPS)
+    gsem, lsem, ss1, rs1, ss2, rs2, sa, ra_sem, sx, rx_sem, sz, rz_sem, sf, rf_sem = scratch
 
     f, t = lax.axis_index("fsdp"), lax.axis_index("tp")
     line, part = f // 2, f % 2
@@ -91,7 +89,8 @@
     names.start()
     loads = [pltpu.make_async_copy(g_hbm.at[:, c * BLOCK : (c + 1) * BLOCK], gv.at[c], gsem.at[c]) for c in range(COLS)]
     big = [
-        pltpu.make_async_copy(lr_hbm, lr, lsem.at[0]),
+        pltpu.make_async_copy(lr_hbm.at[:, :, r], lr.at[r], lsem.at[5 + r]) for r in range(GROUPS)
+    ] + [
         pltpu.make_async_copy(rr_hbm, rr, lsem.at[1]),
         pltpu.make_async_copy(ls_hbm, nl, lsem.at[2]),
         pltpu.make_async_copy(rs_hbm, nr, lsem.at[3]),
@@ -141,6 +140,20 @@
     lines = [jnp.maximum(slots[d], 0) for d in ts]
     my_line = jnp.maximum(mine, 0)
 
+    def cut_rows(r, factor):
+        for h in range(2):
+            for p in range(N_T):
+                start = r * TILE + (h * N_T + p) * RW
+                rows = full[start : start + RW]
+                s[h, p, r * RW : (r + 1) * RW] = (rows if factor is None else rows * factor).astype(bf16)
+
+    def spread(c):
+        r, c0, width = BACK[c]
+        rows, cut = pl.ds(r * RW, RW), pl.ds(c0, width)
+        for i, d in enumerate(ts):
+            send(s.at[:, d, rows, cut], ra[c].at[t], sa.at[c], ra_sem.at[c], f, d)
+        ra[c][t] = s[:, t, rows, cut]
+
     def turn(m):
         pair = slice(m * PAIR, (m + 1) * PAIR)
         gt[pair, :] = g[:, :, :, pair].reshape(BLOCK, PAIR).T
@@ -150,7 +163,7 @@
         for k, (c0, _, _) in enumerate(CHUNKS):
             if c0 // PAIR == m:
                 drain(s2[k], rs2.at[k])
-        h = jnp.dot(lr[...], g[:, :, :, pair].reshape(BLOCK, PAIR), preferred_element_type=f32).astype(bf16)
+        h = jnp.dot(lr[...].reshape(BLOCK, BLOCK), g[:, :, :, pair].reshape(BLOCK, PAIR), preferred_element_type=f32).astype(bf16)
         total = jnp.zeros((8, TILE), f32)
         for i in range(BLOCK // TILE):
             rows = slice(i * TILE, (i + 1) * TILE)
@@ -160,7 +173,11 @@
                 if m:
                     p += full[rows, cut]
                 full[rows, cut] = p
-                total += jnp.sum((p * p).reshape(TILE // 8, 8, TILE), axis=0)
+                if m == BLOCK // PAIR - 1:
+                    total += jnp.sum((p * p).reshape(TILE // 8, 8, TILE), axis=0)
+            if m == BLOCK // PAIR - 1 and i == 0:
+                cut_rows(0, None)
+                spread(0)
         return total
 
     for k, (c0, r0, n) in enumerate(CHUNKS):
@@ -170,26 +187,31 @@
             send(s2[k].at[i], g.at[:, t, pl.ds(r0, n), c0 : c0 + CW], ss2.at[k], rs2.at[k], f, d)
         g[:, t, r0 : r0 + n, c0 : c0 + CW] = r1[k][my_line]
         if k == 4:
-            for load in big[:2]:
+            for load in big[:5]:
                 load.wait()
-        if k in (5, 7, 9):
-            products((k - 5) // 2)
-            turn((k - 5) // 2)
+        for m in range(BLOCK // PAIR - 1):
+            if k == max(j for j in range(FWD) if CHUNKS[j][0] // PAIR == m) + 3:
+                products(m)
+                turn(m)
     total = products(BLOCK // PAIR - 1)
-    factor = lax.rsqrt(jnp.sum(total) / (BLOCK * BLOCK) + eps)
-
-    for r in range(GROUPS):
-        for h in range(2):
-            for p in range(N_T):
-                start = h * (BLOCK // 2) + p * ROWS + r * RW
-                s[h, p, r * RW : (r + 1) * RW] = (full[start : start + RW] * factor).astype(bf16)
-        rows = pl.ds(r * RW, RW)
-        for e in range(HALVES):
-            c = r * HALVES + e
-            cut = pl.ds(e * HW, HW)
-            for i, d in enumerate(ts):
-                send(s.at[:, d, rows, cut], ra[c].at[t], sa.at[c], ra_sem.at[c], f, d)
-            ra[c][t] = s[:, t, rows, cut]
+    factor = lax.rsqrt(jnp.sum(total, axis=(0, 1), keepdims=True) / (BLOCK * BLOCK) + eps)
+
+    fac_out[...] = jnp.broadcast_to(factor, fac_out.shape)
+    for d in ts:
+        send(fac_out, fac.at[t], sf, rf_sem, f, d)
+    fac[t] = jnp.broadcast_to(factor, fac_out.shape)
+    for c in range(1, BWD):
+        r, c0, _ = BACK[c]
+        if r and not c0:
+            cut_rows(r, factor)
+        spread(c)
+
+    def scaled(piece, slot, c):
+        if BACK[c][0]:
+            return piece
+        scale = jnp.concatenate([fac[slot][0:1]] * (BACK[c][2] // 128), axis=1)
+        return (piece.astype(f32) * scale).astype(bf16)
+
 
     def left(i):
         rows = pl.ds(i * TILE, TILE)
@@ -208,7 +230,7 @@
             nr[rows, cut] = decay * nr[rows, cut] + jnp.where(has, (1.0 - decay) * p, 0.0)
 
     turn(BLOCK // PAIR - 1)
-    for load in big[2:]:
+    for load in big[5:]:
         load.wait()
     work = [lambda i=i: left(i) for i in range(4)] + [lambda i=i: right(i) for i in range(4)]
     work.pop(0)()
@@ -227,8 +249,9 @@
     my_parts = parts_of(t)
 
     def finish(r):
-        for e in range(HALVES):
-            drain(b2.at[r * HALVES + e], rx_sem.at[r * HALVES + e])
+        for c in range(BWD):
+            if BACK[c][0] == r:
+                drain(b2[c], rx_sem.at[c])
         here = pl.ds(pl.multiple_of(t * ROWS + r * RW, RW), RW)
         for i, d in enumerate(ts):
             for j, (source, q) in enumerate(parts[i]):
@@ -237,18 +260,20 @@
         for j, (source, q) in enumerate(my_parts):
             upd[here, j * Q : (j + 1) * Q] = rx[r][source, q]
 
-    for c in range(BWD):
-        r, e = c // HALVES, c % HALVES
+    for c, (r, c0, width) in enumerate(BACK):
         drain(ra[c].at[pl.ds(0, NT)], ra_sem.at[c])
+        if c == 0:
+            drain(fac.at[pl.ds(0, NT)], rf_sem)
+        first, count = c0 // Q, width // Q
         for i, d in enumerate(fs):
-            piece = ra[c][sources[i], d % 2]
-            for q in range(QH):
-                b2[c, i, q] = piece[:, q * Q : (q + 1) * Q]
-            send(b2.at[c, i], rx[r].at[f, pl.ds(e * QH, QH)], sx.at[c], rx_sem.at[c], d, t)
-        piece = ra[c][my_source, part]
-        for q in range(QH):
-            rx[r][f, e * QH + q] = piece[:, q * Q : (q + 1) * Q]
-        if e == HALVES - 1 and r > 0:
+            piece = scaled(ra[c][sources[i], d % 2], sources[i], c)
+            for q in range(count):
+                b2[c][i, q] = piece[:, q * Q : (q + 1) * Q]
+            send(b2[c].at[i], rx[r].at[f, pl.ds(first, count)], sx.at[c], rx_sem.at[c], d, t)
+        piece = scaled(ra[c][my_source, part], my_source, c)
+        for q in range(count):
+            rx[r][f, first + q] = piece[:, q * Q : (q + 1) * Q]
+        if r and c0 + width == BLOCK:
             finish(r - 1)
         if work:
             work.pop(0)()
@@ -259,7 +284,8 @@
         drain(s2[k], ss2.at[k])
     for c in range(BWD):
         drain(ra[c].at[pl.ds(0, NT)], sa.at[c])
-        drain(b2.at[c], sx.at[c])
+        drain(b2[c], sx.at[c])
+    drain(fac.at[pl.ds(0, NT)], sf)
     for r in range(GROUPS):
         drain(b3.at[r], sz.at[r])
         drain(b3.at[r], rz_sem.at[r])
@@ -279,26 +305,29 @@
         out_specs=[vmem] * 3,
         scratch_shapes=[
             VMEM((COLS, ROWS, BLOCK), bf16),
-            VMEM((BLOCK, BLOCK), bf16),
+            VMEM((GROUPS, 2, N_T, RW, BLOCK), bf16),
             VMEM((BLOCK, BLOCK), bf16),
             VMEM((2, N_T, ROWS, BLOCK), bf16),
             VMEM((BLOCK, BLOCK), bf16),
             VMEM((BLOCK, BLOCK), f32),
             VMEM((2, N_T, ROWS, BLOCK), bf16),
-            VMEM((BWD, NF, QH, RW, Q), bf16),
             VMEM((GROUPS, NT, RW, OUT_COLS), bf16),
+            VMEM((N_T, 8, 128), f32),
+            VMEM((8, 128), f32),
             pltpu.SMEM((LINES * COLS,), jnp.int32),
             pltpu.SMEM((N_T + LINES,), jnp.int32),
         ]
         + [VMEM((NF, n, CW), bf16) for _, _, n in CHUNKS]
         + [VMEM((NT, 2, n, CW), bf16) for _, _, n in CHUNKS]
         + [VMEM((LINES, 2, n, CW), bf16) for _, _, n in CHUNKS]
-        + [VMEM((N_T, 2, RW, HW), bf16)] * BWD
+        + [VMEM((N_T, 2, RW, w), bf16) for _, _, w in BACK]
+        + [VMEM((NF, w // Q, RW, Q), bf16) for _, _, w in BACK]
         + [VMEM((N_F, BLOCK // Q, RW, Q), bf16)] * GROUPS
-        + [DMA((COLS,)), DMA((5,))]
+        + [DMA((COLS,)), DMA((5 + GROUPS,))]
         + [DMA((FWD,))] * 4
         + [DMA((BWD,))] * 4
-        + [DMA((GROUPS,))] * 2,
+        + [DMA((GROUPS,))] * 2
+        + [DMA] * 2,
         compiler_params=pltpu.CompilerParams(collective_id=0, has_side_effects=True, vmem_limit_bytes=40 << 20),
         name="shampoo",
     )(owner, gradient, l_stat, r_stat, l_root, r_root)
@@ -326,7 +355,8 @@
 
 
 def per_device(gradient, owner, l_stat, r_stat, l_root, r_root):
-    args = [pltpu.with_memory_space_constraint(x, pltpu.HBM) for x in (owner, gradient, l_stat[0], r_stat[0], l_root[0], r_root[0])]
+    args = (owner, gradient, l_stat[0], r_stat[0], l_root.reshape(2, N_T, GROUPS, RW, BLOCK), r_root[0])
+    args = [pltpu.with_memory_space_constraint(x, pltpu.HBM) for x in args]
     update, new_left, new_right = write(*step(*args))
     return (update, new_left[None], new_right[None])
 

time: 85.4 us -> 84.6 us (level)
  no operation moved by 1% of the time
where the time goes in v4:
time: 84.6 us; the launch traced here: 84.5 us
  Pallas kernels  83.7 us (99%)
    pallas_call x1, Pallas kernels, step(): pl.pallas_call(kernel, out_shape=[VMEM((N_T * ROWS, OUT_COLS), bf16), VME...  79.8 us
    pallas_call x1, Pallas kernels, write(): pl.pallas_call(write_kernel, out_shape=[jax.ShapeDtypeStruct(x.shape, x.d...  3.85 us

profile of v4, /device:TPU:1, one launch (start us, length us, event | category | flops | bytes accessed | tf_op | source)
XLA Modules:
  0.0 84.5 jit_solution(8499046105086667690)
XLA Ops:
  0.6 79.8 %shampoo.1 = (bf16[512,1280]{1,0:T(8,128)(2,1)S(1)}, f32[1024,1024]{1,0:T(8,128)S(1)}, f32[1024,1024]{1,0:T(8,128)S(1)}) custom-call(s32[80]{0:T(128)} %owner_hbm.1, bf16[64,10240]{1,0:T(8,128)(2,1)} %g_hbm.1, f32[1024,1024]{1,0:T(8,128)} %bitcast.6, f32[1024,1024]{1,0:T(8,128)} %bitcast.7, bf16[2,8,4,16,1024]{4,3,2,1,0:T(8,128)(2,1)} %bitcast.8, ...), custom_call_target="tpu_custom_call" | custom-call | tf_op jit(solution)/shard_map/shampoo/pallas_call | solution.py:297
  80.5 3.9 %write.1 = (bf16[512,1280]{1,0:T(8,128)(2,1)}, f32[1024,1024]{1,0:T(8,128)}, f32[1024,1024]{1,0:T(8,128)}) custom-call(bf16[512,1280]{1,0:T(8,128)(2,1)S(1)} %get-tuple-element.9.a, f32[1024,1024]{1,0:T(8,128)S(1)} %get-tuple-element.10.b, f32[1024,1024]{1,0:T(8,128)S(1)} %get-tuple-element.11.c), custom_call_target="tpu_custom_call" | custom-call | tf_op jit(solution)/shard_map/write/pallas_call | solution.py:346

commit v5 on v4

--- a/solution.py
+++ b/solution.py
@@ -25,6 +25,7 @@
 CHUNKS += [(c, 0, 64) for c in range(CW, BLOCK - CW, CW)]
 CHUNKS += [(BLOCK - CW, 0, 32), (BLOCK - CW, 32, 32)]
 FWD = len(CHUNKS)
+STAGED = 2
 PAIR = 256
 RW = 16
 GROUPS = ROWS // RW
@@ -79,14 +80,14 @@
     fs = [fsdp_at(f, step) for step in F_STEPS]
     ts = [tp_at(t, step) for step in T_STEPS]
 
+    names = pltpu.make_async_copy(owner_hbm, owner_ref, lsem.at[4])
+    names.start()
     barrier = pltpu.get_barrier_semaphore()
     for d in fs:
         pl.semaphore_signal(barrier, inc=1, device_id=(d, t), device_id_type=MESH)
     for d in ts:
         pl.semaphore_signal(barrier, inc=1, device_id=(f, d), device_id_type=MESH)
 
-    names = pltpu.make_async_copy(owner_hbm, owner_ref, lsem.at[4])
-    names.start()
     loads = [pltpu.make_async_copy(g_hbm.at[:, c * BLOCK : (c + 1) * BLOCK], gv.at[c], gsem.at[c]) for c in range(COLS)]
     big = [
         pltpu.make_async_copy(lr_hbm.at[:, :, r], lr.at[r], lsem.at[5 + r]) for r in range(GROUPS)
@@ -109,15 +110,23 @@
 
     cols = [column_of(d) for d in fs]
     my_col = column_of(f)
-    pl.semaphore_wait(barrier, NF + NT)
     for load in loads:
         load.wait()
 
-    for k, (c0, r0, n) in enumerate(CHUNKS):
+    def stage(k):
+        c0, r0, n = CHUNKS[k]
+        for i in range(NF):
+            s1[k][i] = gv[cols[i], r0 : r0 + n, c0 : c0 + CW]
+        r1[k][line, part] = gv[my_col, r0 : r0 + n, c0 : c0 + CW]
+
+    for k in range(STAGED):
+        stage(k)
+    pl.semaphore_wait(barrier, NF + NT)
+    for k in range(FWD):
+        if k >= STAGED:
+            stage(k)
         for i, d in enumerate(fs):
-            s1[k][i] = gv[cols[i], r0 : r0 + n, c0 : c0 + CW]
             send(s1[k].at[i], r1[k].at[line, part], ss1.at[k], rs1.at[k], d, t)
-        r1[k][line, part] = gv[my_col, r0 : r0 + n, c0 : c0 + CW]
         if k == 1:
             for load in big:
                 load.start()
@@ -163,19 +172,26 @@
         for k, (c0, _, _) in enumerate(CHUNKS):
             if c0 // PAIR == m:
                 drain(s2[k], rs2.at[k])
-        h = jnp.dot(lr[...].reshape(BLOCK, BLOCK), g[:, :, :, pair].reshape(BLOCK, PAIR), preferred_element_type=f32).astype(bf16)
+        block = g[:, :, :, pair].reshape(BLOCK, PAIR)
+        final = m == BLOCK // PAIR - 1
+        if not final:
+            h = jnp.dot(lr[...].reshape(BLOCK, BLOCK), block, preferred_element_type=f32).astype(bf16)
         total = jnp.zeros((8, TILE), f32)
         for i in range(BLOCK // TILE):
             rows = slice(i * TILE, (i + 1) * TILE)
+            if final:
+                part_h = jnp.dot(lr[i].reshape(TILE, BLOCK), block, preferred_element_type=f32).astype(bf16)
+            else:
+                part_h = h[rows]
             for j in range(BLOCK // TILE):
                 cut = slice(j * TILE, (j + 1) * TILE)
-                p = jnp.dot(h[rows], rr[pair, cut], preferred_element_type=f32)
+                p = jnp.dot(part_h, rr[pair, cut], preferred_element_type=f32)
                 if m:
                     p += full[rows, cut]
                 full[rows, cut] = p
-                if m == BLOCK // PAIR - 1:
+                if final:
                     total += jnp.sum((p * p).reshape(TILE // 8, 8, TILE), axis=0)
-            if m == BLOCK // PAIR - 1 and i == 0:
+            if final and i == 0:
                 cut_rows(0, None)
                 spread(0)
         return total

time: 84.6 us -> 83.9 us (level)
  no operation moved by 1% of the time
where the time goes in v5:
time: 83.9 us; the launch traced here: 83.8 us
  Pallas kernels  83 us (99%)
    pallas_call x1, Pallas kernels, step(): pl.pallas_call(kernel, out_shape=[VMEM((N_T * ROWS, OUT_COLS), bf16), VME...  79.2 us
    pallas_call x1, Pallas kernels, write(): pl.pallas_call(write_kernel, out_shape=[jax.ShapeDtypeStruct(x.shape, x.d...  3.85 us

profile of v5, /device:TPU:1, one launch (start us, length us, event | category | flops | bytes accessed | tf_op | source)
XLA Modules:
  0.0 83.8 jit_solution(7039186854211040834)
XLA Ops:
  0.6 79.2 %shampoo.1 = (bf16[512,1280]{1,0:T(8,128)(2,1)S(1)}, f32[1024,1024]{1,0:T(8,128)S(1)}, f32[1024,1024]{1,0:T(8,128)S(1)}) custom-call(s32[80]{0:T(128)} %owner_hbm.1, bf16[64,10240]{1,0:T(8,128)(2,1)} %g_hbm.1, f32[1024,1024]{1,0:T(8,128)} %bitcast.6, f32[1024,1024]{1,0:T(8,128)} %bitcast.7, bf16[2,8,4,16,1024]{4,3,2,1,0:T(8,128)(2,1)} %bitcast.8, ...), custom_call_target="tpu_custom_call" | custom-call | tf_op jit(solution)/shard_map/shampoo/pallas_call | solution.py:313
  79.8 3.9 %write.1 = (bf16[512,1280]{1,0:T(8,128)(2,1)}, f32[1024,1024]{1,0:T(8,128)}, f32[1024,1024]{1,0:T(8,128)}) custom-call(bf16[512,1280]{1,0:T(8,128)(2,1)S(1)} %get-tuple-element.9.a, f32[1024,1024]{1,0:T(8,128)S(1)} %get-tuple-element.10.b, f32[1024,1024]{1,0:T(8,128)S(1)} %get-tuple-element.11.c), custom_call_target="tpu_custom_call" | custom-call | tf_op jit(solution)/shard_map/write/pallas_call | solution.py:362

commit v6 on v5

--- a/solution.py
+++ b/solution.py
@@ -38,6 +38,9 @@
 F_STEPS = [(2, 2), (1, 2), (2, 1), (3, 2), (2, 3), (1, 1), (3, 3), (1, 3), (3, 1), (0, 2), (2, 0), (0, 1), (1, 0), (0, 3), (3, 0)]
 T_STEPS = [(2, 0), (2, 1), (1, 0), (3, 0), (1, 1), (3, 1), (0, 1)]
 NF, NT = len(F_STEPS), len(T_STEPS)
+Z_STEPS = [(2, 0), (1, 0), (3, 0)]
+NZ = len(Z_STEPS)
+DIRECT = 2
 
 
 def fsdp_at(f, step):
@@ -72,13 +75,16 @@
         return taken
 
     gv, lr, rr, g, gt, full, s, b3, fac, fac_out, owner_ref, slots = take(12)
-    s1, s2, r1, ra, b2, rx = take(FWD), take(FWD), take(FWD), take(BWD), take(BWD), take(GROUPS)
-    gsem, lsem, ss1, rs1, ss2, rs2, sa, ra_sem, sx, rx_sem, sz, rz_sem, sf, rf_sem = scratch
+    s1, s2, r1, ra, rl, b2, rx = take(FWD), take(FWD), take(FWD), take(BWD), take(BWD), take(BWD), take(GROUPS)
+    last = take(GROUPS - 1)
+    gsem, lsem, ss1, rs1, ss2, rs2, sa, ra_sem, sx, rx_sem, sz, rz_sem, sf, rf_sem, sl, rl_sem, sl_last, last_sem = scratch
 
     f, t = lax.axis_index("fsdp"), lax.axis_index("tp")
     line, part = f // 2, f % 2
     fs = [fsdp_at(f, step) for step in F_STEPS]
     ts = [tp_at(t, step) for step in T_STEPS]
+    zs = [tp_at(t, step) for step in Z_STEPS]
+    other = tp_at(t, (0, 1))
 
     names = pltpu.make_async_copy(owner_hbm, owner_ref, lsem.at[4])
     names.start()
@@ -159,9 +165,20 @@
     def spread(c):
         r, c0, width = BACK[c]
         rows, cut = pl.ds(r * RW, RW), pl.ds(c0, width)
-        for i, d in enumerate(ts):
+        for j, d in enumerate(zs):
+            if c < DIRECT:
+                send(s.at[:, d + other - t, rows, cut], ra[c].at[t], sa.at[c], ra_sem.at[c], f, d + other - t)
+            else:
+                send(s.at[:, d + other - t, rows, cut], rl[c].at[j], sl.at[c], rl_sem.at[c], f, other)
+        send(s.at[:, other, rows, cut], ra[c].at[t], sa.at[c], ra_sem.at[c], f, other)
+        for d in zs:
             send(s.at[:, d, rows, cut], ra[c].at[t], sa.at[c], ra_sem.at[c], f, d)
         ra[c][t] = s[:, t, rows, cut]
+
+    def relay(c):
+        drain(rl[c], rl_sem.at[c])
+        for j, d in enumerate(zs):
+            send(rl[c].at[j], ra[c].at[other], sa.at[c], ra_sem.at[c], f, d)
 
     def turn(m):
         pair = slice(m * PAIR, (m + 1) * PAIR)
@@ -221,6 +238,9 @@
         if r and not c0:
             cut_rows(r, factor)
         spread(c)
+        if c > DIRECT:
+            relay(c - 1)
+    relay(BWD - 1)
 
     def scaled(piece, slot, c):
         if BACK[c][0]:
@@ -272,9 +292,19 @@
         for i, d in enumerate(ts):
             for j, (source, q) in enumerate(parts[i]):
                 b3[r, i, :, j * Q : (j + 1) * Q] = rx[r][source, q]
-            send(b3.at[r, i], upd.at[here], sz.at[r], rz_sem.at[r], f, d)
+            z, core = T_STEPS[i]
+            if core and z and r < GROUPS - 1:
+                send(b3.at[r, i], last[r].at[Z_STEPS.index((z, 0))], sz.at[r], last_sem.at[r], f, other)
+            else:
+                send(b3.at[r, i], upd.at[here], sz.at[r], rz_sem.at[r], f, d)
         for j, (source, q) in enumerate(my_parts):
             upd[here, j * Q : (j + 1) * Q] = rx[r][source, q]
+
+    def relay_last(r):
+        drain(last[r], last_sem.at[r])
+        there = pl.ds(pl.multiple_of(other * ROWS + r * RW, RW), RW)
+        for j, d in enumerate(zs):
+            send(last[r].at[j], upd.at[there], sl_last.at[r], rz_sem.at[r], f, d)
 
     for c, (r, c0, width) in enumerate(BACK):
         drain(ra[c].at[pl.ds(0, NT)], ra_sem.at[c])
@@ -291,6 +321,7 @@
             rx[r][f, first + q] = piece[:, q * Q : (q + 1) * Q]
         if r and c0 + width == BLOCK:
             finish(r - 1)
+            relay_last(r - 1)
         if work:
             work.pop(0)()
     finish(GROUPS - 1)
@@ -300,8 +331,12 @@
         drain(s2[k], ss2.at[k])
     for c in range(BWD):
         drain(ra[c].at[pl.ds(0, NT)], sa.at[c])
+        if c >= DIRECT:
+            drain(rl[c], sl.at[c])
         drain(b2[c], sx.at[c])
     drain(fac.at[pl.ds(0, NT)], sf)
+    for r in range(GROUPS - 1):
+        drain(last[r], sl_last.at[r])
     for r in range(GROUPS):
         drain(b3.at[r], sz.at[r])
         drain(b3.at[r], rz_sem.at[r])
@@ -337,13 +372,17 @@
         + [VMEM((NT, 2, n, CW), bf16) for _, _, n in CHUNKS]
         + [VMEM((LINES, 2, n, CW), bf16) for _, _, n in CHUNKS]
         + [VMEM((N_T, 2, RW, w), bf16) for _, _, w in BACK]
+        + [VMEM((NZ, 2, RW, w), bf16) for _, _, w in BACK]
         + [VMEM((NF, w // Q, RW, Q), bf16) for _, _, w in BACK]
         + [VMEM((N_F, BLOCK // Q, RW, Q), bf16)] * GROUPS
+        + [VMEM((NZ, RW, OUT_COLS), bf16)] * (GROUPS - 1)
         + [DMA((COLS,)), DMA((5 + GROUPS,))]
         + [DMA((FWD,))] * 4
         + [DMA((BWD,))] * 4
         + [DMA((GROUPS,))] * 2
-        + [DMA] * 2,
+        + [DMA] * 2
+        + [DMA((BWD,))] * 2
+        + [DMA((GROUPS,))] * 2,
         compiler_params=pltpu.CompilerParams(collective_id=0, has_side_effects=True, vmem_limit_bytes=40 << 20),
         name="shampoo",
     )(owner, gradient, l_stat, r_stat, l_root, r_root)

time: 83.9 us -> 84.2 us (level)
  no operation moved by 1% of the time
where the time goes in v6:
time: 84.2 us; the launch traced here: 84 us
  Pallas kernels  83.2 us (99%)
    pallas_call x1, Pallas kernels, step(): pl.pallas_call(kernel, out_shape=[VMEM((N_T * ROWS, OUT_COLS), bf16), VME...  79.4 us
    pallas_call x1, Pallas kernels, write(): pl.pallas_call(write_kernel, out_shape=[jax.ShapeDtypeStruct(x.shape, x.d...  3.85 us

profile of v6, /device:TPU:1, one launch (start us, length us, event | category | flops | bytes accessed | tf_op | source)
XLA Modules:
  0.0 84.0 jit_solution(11485431325268615833)
XLA Ops:
  0.6 79.4 %shampoo.1 = (bf16[512,1280]{1,0:T(8,128)(2,1)S(1)}, f32[1024,1024]{1,0:T(8,128)S(1)}, f32[1024,1024]{1,0:T(8,128)S(1)}) custom-call(s32[80]{0:T(128)} %owner_hbm.1, bf16[64,10240]{1,0:T(8,128)(2,1)} %g_hbm.1, f32[1024,1024]{1,0:T(8,128)} %bitcast.6, f32[1024,1024]{1,0:T(8,128)} %bitcast.7, bf16[2,8,4,16,1024]{4,3,2,1,0:T(8,128)(2,1)} %bitcast.8, ...), custom_call_target="tpu_custom_call" | custom-call | tf_op jit(solution)/shard_map/shampoo/pallas_call | solution.py:348
  80.0 3.9 %write.1 = (bf16[512,1280]{1,0:T(8,128)(2,1)}, f32[1024,1024]{1,0:T(8,128)}, f32[1024,1024]{1,0:T(8,128)}) custom-call(bf16[512,1280]{1,0:T(8,128)(2,1)S(1)} %get-tuple-element.9.a, f32[1024,1024]{1,0:T(8,128)S(1)} %get-tuple-element.10.b, f32[1024,1024]{1,0:T(8,128)S(1)} %get-tuple-element.11.c), custom_call_target="tpu_custom_call" | custom-call | tf_op jit(solution)/shard_map/write/pallas_call | solution.py:401
